TPU v7x, 256 devices: a whole 4x4x8 slice. The times are simulated.
256 devices in a mesh: row: 16 (over z, core), col: 16 (over y, x).
Axes of the slice: x: 4, y: 4, z: 8, core: 2. Of those that a mesh axis runs over, the one named last changes fastest.
Arguments:
- momentum: bfloat16 [8192, 26624], P('row', 'col'), may hold values from -6 to 6
- gradient: bfloat16 [8192, 26624], P('row', 'col'), may hold values from -180 to 180
- right_factor: bfloat16 [26624, 512], P('col'), may hold values from -6 to 6
Outputs:
- new_momentum: bfloat16 [8192, 26624], P('row', 'col')
- weight_update: bfloat16 [8192, 26624], P('row', 'col')
- new_factor: float32 [26624, 512], P('col')
All inputs are finite; a program needn't handle non-finite values.
Results may differ from a plain program's by a relative error of at most 0.013.
Values may be sent and summed in bfloat16 or wider, within the bound.
No kernel may reach another device: no remote copies, remote signals or barrier semaphores. Data moves between devices by JAX's collectives and lax.ppermute only.
A program may use at most 64 MiB of HBM per device.

v0:
```python
import math

import jax
import jax.numpy as jnp
from jax import lax
from jax.experimental import pallas as pl
from jax.experimental.pallas import tpu as pltpu
from jax.sharding import PartitionSpec as P

ROWS = 8192
COLS = 26624
RANK = 512


NORM_EPS = 1e-06
GRAM_JITTER = 0.0001
FEEDBACK = 0.25

HIGHEST = lax.Precision.HIGHEST
BLOCK = 128
BLOCKS = RANK // BLOCK
SUB = 8
GROUPS = BLOCK // SUB
PAIRS = [(i, j) for i in range(BLOCKS) for j in range(i, BLOCKS)]


def sub_row(x, k):
    return jnp.broadcast_to(x[k : k + 1, :], (SUB, BLOCK))


def lane_col(x, c):
    return jnp.broadcast_to(x[:, c : c + 1], (SUB, BLOCK))


def pieces(x):
    hi = x.astype(jnp.bfloat16)
    rest = x - hi.astype(jnp.float32)
    mid = rest.astype(jnp.bfloat16)
    return hi, mid, (rest - mid.astype(jnp.float32)).astype(jnp.bfloat16)


def stacked(*parts):
    return jnp.concatenate([x.astype(jnp.float32) for x in parts], axis=0).astype(jnp.bfloat16)


def factor_block(rows):
    sub = lax.broadcasted_iota(jnp.int32, (SUB, BLOCK), 0)
    lane = lax.broadcasted_iota(jnp.int32, (SUB, BLOCK), 1)
    out = []
    for p in range(GROUPS):
        panel = (lane >= SUB * p) & (lane < SUB * (p + 1))
        cols = [lane_col(rows[p], SUB * p + j) for j in range(SUB)]
        x = jnp.where(panel, jnp.where(lane == sub + SUB * p, 1.0, 0.0), rows[p])
        pivots, recips, row_k, upper = [], [], [], []
        for k in range(SUB):
            pivot = sub_row(cols[k], k)
            r = pl.reciprocal(pivot, approx=True)
            m = jnp.where(sub > k, cols[k] * r, 0.0)
            u = {j: sub_row(cols[j], k) for j in range(k + 1, SUB)}
            for j in range(k + 1, SUB):
                cols[j] = cols[j] - m * u[j]
            xk = sub_row(x, k)
            if k < SUB - 1:
                x = x - m * xk
            pivots.append(pivot)
            recips.append(r)
            row_k.append(xk)
            upper.append(u)
        d8 = pivots[0]
        for k in range(1, SUB):
            d8 = jnp.where(sub == k, pivots[k], d8)
        out.append(jnp.where(lane < SUB * (p + 1), x * lax.rsqrt(d8), 0.0))
        if p + 1 < GROUPS:
            b = [lane_col(rows[p + 1], SUB * p + j) for j in range(SUB)]
            y = jnp.where(panel, 0.0, rows[p + 1])
            for k in range(SUB):
                m = b[k] * recips[k]
                for j in range(k + 1, SUB):
                    b[j] = b[j] - m * upper[k][j]
                y = y - m * row_k[k]
            rows[p + 1] = y
        if p + 2 < GROUPS:
            r8 = recips[0]
            for k in range(1, SUB):
                r8 = jnp.where(sub == k, recips[k], r8)
            hi, mid, low = pieces(x)
            hi2, mid2, low2 = pieces(x * r8)
            product = lax.dot_general(
                stacked(hi, hi, mid, mid, hi, low),
                stacked(hi2, mid2, hi2, mid2, low2, hi2),
                (((0,), (0,)), ((), ())),
                preferred_element_type=jnp.float32,
            )
            for q in range(p + 2, GROUPS):
                rows[q] = jnp.where(panel, 0.0, rows[q]) - product[SUB * q : SUB * (q + 1), :]
    return out


def inverse_factor_kernel(core_ref, mine_ref, theirs_ref, m_ref, s_ref, d_ref, x_ref, y_ref):
    half = mine_ref.shape[0]

    def gram(n):
        return jnp.where(core_ref[0] == n // half, mine_ref[n % half], theirs_ref[n % half])

    eye = (
        lax.broadcasted_iota(jnp.int32, (BLOCK, BLOCK), 0)
        == lax.broadcasted_iota(jnp.int32, (BLOCK, BLOCK), 1)
    )
    diagonal = jnp.zeros((BLOCK, BLOCK), jnp.float32)
    for n, (i, j) in enumerate(PAIRS):
        if i == j:
            diagonal += jnp.where(eye, gram(n), 0.0)
    jitter = (GRAM_JITTER / RANK) * jnp.sum(diagonal)
    s_ref[...] = jnp.zeros_like(s_ref)
    for n, (i, j) in enumerate(PAIRS):
        x = gram(n)
        if i == j:
            x = x + jnp.where(eye, jitter, 0.0)
        s_ref[BLOCK * i : BLOCK * (i + 1), BLOCK * j : BLOCK * (j + 1)] = x

    def block(b, carry):
        lo = pl.multiple_of(b * BLOCK, BLOCK)
        rows = [s_ref[pl.ds(lo + SUB * q, SUB), pl.ds(lo, BLOCK)] for q in range(GROUPS)]
        for q, x in enumerate(factor_block(rows)):
            d_ref[SUB * q : SUB * (q + 1), :] = x
        m_bb = d_ref[...]
        hi, mid, low = pieces(m_bb)
        first = jnp.concatenate([hi, hi, mid, mid, hi, low], axis=1)
        hi, mid, low = pieces(s_ref[pl.ds(lo, BLOCK), :])
        second = jnp.concatenate([hi, mid, hi, mid, low, hi], axis=0)
        s_ref[pl.ds(lo, BLOCK), :] = jnp.dot(first, second, preferred_element_type=jnp.float32)
        s_ref[pl.ds(lo, BLOCK), pl.ds(lo, BLOCK)] = m_bb
        hi, mid, low = pieces(s_ref[pl.ds(lo, BLOCK), :])
        for n, (x, y) in enumerate(((hi, hi), (hi, mid), (mid, hi), (mid, mid), (hi, low), (low, hi))):
            x_ref[BLOCK * n : BLOCK * (n + 1), :] = x
            y_ref[BLOCK * n : BLOCK * (n + 1), :] = y
        for i in range(1, BLOCKS):

            @pl.when(i > b)
            def _():
                here = slice(BLOCK * i, BLOCK * (i + 1))
                s_ref[here, pl.ds(lo, BLOCK)] = jnp.zeros((BLOCK, BLOCK), jnp.float32)
                s_ref[here, :] -= lax.dot_general(
                    x_ref[:, here], y_ref[...], (((0,), (0,)), ((), ())), preferred_element_type=jnp.float32
                )

        return carry

    lax.fori_loop(0, BLOCKS, block, 0)
    for i in range(BLOCKS):
        for j in range(BLOCKS):
            here = (slice(BLOCK * i, BLOCK * (i + 1)), slice(BLOCK * j, BLOCK * (j + 1)))
            m_ref[here] = s_ref[here] if j <= i else jnp.zeros((BLOCK, BLOCK), jnp.float32)


def gram_kernel(p_ref, o_ref):
    for i in range(BLOCKS):
        rows = lax.dot_general(
            p_ref[:, BLOCK * i : BLOCK * (i + 1)],
            p_ref[:, BLOCK * i :],
            (((0,), (0,)), ((), ())),
            precision=HIGHEST,
            preferred_element_type=jnp.float32,
        )
        for j in range(i, BLOCKS):
            o_ref[PAIRS.index((i, j))] = rows[:, BLOCK * (j - i) : BLOCK * (j - i + 1)]


def gram_blocks(projected):
    return pl.pallas_call(
        gram_kernel,
        out_shape=jax.ShapeDtypeStruct((len(PAIRS), BLOCK, BLOCK), jnp.float32),
        in_specs=[pl.BlockSpec(memory_space=pltpu.VMEM)],
        out_specs=pl.BlockSpec(memory_space=pltpu.VMEM),
        compiler_params=pltpu.CompilerParams(vmem_limit_bytes=16 * 1024 * 1024),
        cost_estimate=pl.CostEstimate(flops=2**31, bytes_accessed=2**21, transcendentals=0),
    )(projected)


def inverse_factor(core, mine, theirs):
    return pl.pallas_call(
        inverse_factor_kernel,
        out_shape=jax.ShapeDtypeStruct((RANK, RANK), jnp.float32),
        in_specs=[pl.BlockSpec(memory_space=pltpu.SMEM)] + [pl.BlockSpec(memory_space=pltpu.VMEM)] * 2,
        out_specs=pl.BlockSpec(memory_space=pltpu.VMEM),
        scratch_shapes=[
            pltpu.VMEM((RANK, RANK), jnp.float32),
            pltpu.VMEM((BLOCK, BLOCK), jnp.float32),
            pltpu.VMEM((6 * BLOCK, RANK), jnp.bfloat16),
            pltpu.VMEM((6 * BLOCK, RANK), jnp.bfloat16),
        ],
        compiler_params=pltpu.CompilerParams(vmem_limit_bytes=16 * 1024 * 1024),
        cost_estimate=pl.CostEstimate(flops=25 * 10**9, bytes_accessed=2**21, transcendentals=0),
    )(core.astype(jnp.int32).reshape(1), mine, theirs)


def weights_kernel(half_ref, b_ref, p_ref, *refs):
    *added, o_ref, w_ref = refs
    start = b_ref.shape[1] - w_ref.shape[0]
    half = half_ref[0]
    rows = b_ref[:, pl.ds(pl.multiple_of(half * start, BLOCK), w_ref.shape[0])]
    for n, piece in enumerate(pieces(p_ref[...])):
        term = lax.dot_general(rows, piece, (((0,), (0,)), ((), ())), preferred_element_type=jnp.float32)
        w_ref[...] = term if n == 0 else w_ref[...] + term
    own = w_ref[pl.ds(pl.multiple_of(half * (o_ref.shape[0] - start), SUB), o_ref.shape[0]), :]
    o_ref[...] = own + added[0][...] if added else own


def weights_half(half, blended, projected, *added):
    rows = blended.shape[1] // 2
    start = rows // BLOCK * BLOCK
    vmem = pl.BlockSpec(memory_space=pltpu.VMEM)
    return pl.pallas_call(
        weights_kernel,
        out_shape=jax.ShapeDtypeStruct((rows, RANK), jnp.float32),
        in_specs=[pl.BlockSpec(memory_space=pltpu.SMEM)] + [vmem] * (2 + len(added)),
        out_specs=vmem,
        scratch_shapes=[pltpu.VMEM((blended.shape[1] - start, RANK), jnp.float32)],
        compiler_params=pltpu.CompilerParams(vmem_limit_bytes=32 * 1024 * 1024),
        cost_estimate=pl.CostEstimate(flops=2**31, bytes_accessed=2**22, transcendentals=0),
    )(half.astype(jnp.int32).reshape(1), blended, projected, *added)


def scatter_sum(x, axis, size):
    parts = x.reshape((size, x.shape[0] // size) + x.shape[1:])
    return jnp.sum(lax.all_to_all(parts, axis, 0, 0), axis=0)


def exchange(x, axis, groups, size):
    return lax.all_to_all(jnp.broadcast_to(x, (size,) + x.shape), axis, 0, 0, axis_index_groups=groups)


def local(momentum, gradient, right_factor):
    n_col = lax.axis_size("col")
    n_row = lax.axis_size("row")
    n_z = n_row // 2
    core = lax.axis_index("row") % 2
    other = [(i, i ^ 1) for i in range(n_row)]
    along_z = [[2 * z + c for z in range(n_z)] for c in range(2)]

    def both_halves(mine):
        theirs = lax.ppermute(mine, "row", other)
        return jnp.concatenate([jnp.where(core == 0, mine, theirs), jnp.where(core == 0, theirs, mine)])

    blended = (momentum.astype(jnp.float32) + gradient.astype(jnp.float32)).astype(jnp.bfloat16)
    partial_proj = jnp.dot(blended, right_factor, preferred_element_type=jnp.float32)
    projected = exchange(scatter_sum(partial_proj, "col", n_col), "col", None, n_col).reshape(partial_proj.shape)

    theirs = weights_half(1 - core, blended, projected)
    theirs, projected = lax.optimization_barrier((theirs, projected))
    theirs = lax.ppermute(theirs, "row", other)

    packed = gram_blocks(projected).reshape(2, len(PAIRS) // 2 * BLOCK, BLOCK)
    share = packed.shape[1] // n_col
    here = lax.axis_index("col") * share
    mine, for_other = (
        lax.dynamic_slice(packed, (which, here, 0), (1, share, BLOCK))[0] for which in (core, 1 - core)
    )
    packed = mine + lax.ppermute(for_other, "row", other)

    weights = weights_half(core, blended, projected, theirs)
    weights = lax.psum_scatter(
        weights, "row", scatter_dimension=0, axis_index_groups=along_z, tiled=True
    )
    packed = jnp.sum(exchange(packed, "row", along_z, n_z), axis=0)
    packed = exchange(packed, "col", None, n_col).reshape(len(PAIRS) // 2, BLOCK, BLOCK)

    inverse = inverse_factor(core, packed, lax.ppermute(packed, "row", other))
    left_bf = jnp.dot(
        projected, inverse.T, precision=HIGHEST, preferred_element_type=jnp.float32
    ).astype(jnp.bfloat16)
    left_bf, weights = lax.optimization_barrier((left_bf, weights))
    back_rows = jnp.dot(weights, inverse.T, precision=HIGHEST, preferred_element_type=jnp.float32)
    half = lax.all_gather(
        back_rows.astype(jnp.bfloat16), "row", axis_index_groups=along_z, tiled=True
    )
    squares = jnp.sum(jnp.square(half.astype(jnp.float32)), axis=0).reshape(BLOCKS, BLOCK)
    squares = squares + lax.ppermute(squares, "row", other)
    squares = exchange(squares, "col", None, n_col)
    right_bf = both_halves(half)
    correction = lax.dot_general(
        left_bf, right_bf, (((1,), (1,)), ((), ())), preferred_element_type=jnp.float32
    )
    new_momentum = (blended.astype(jnp.float32) - FEEDBACK * correction).astype(jnp.bfloat16)
    squares, new_momentum = lax.optimization_barrier((squares, new_momentum))
    back_squares = jnp.sum(squares, axis=0).reshape(RANK)
    new_factor = right_bf.astype(jnp.float32) * (1.0 / jnp.sqrt(back_squares / COLS + NORM_EPS))
    factor_bf = new_factor.astype(jnp.bfloat16)
    update_full = lax.dot_general(
        left_bf, factor_bf, (((1,), (1,)), ((), ())), preferred_element_type=jnp.float32
    )
    weight_update = (update_full * math.sqrt(ROWS / RANK)).astype(jnp.bfloat16)
    return (new_momentum, weight_update, new_factor)


def solution(mesh):
    placed = (P("row", "col"), P("row", "col"), P("col", None))
    return jax.shard_map(
        local,
        mesh=mesh,
        in_specs=placed,
        out_specs=(P("row", "col"), P("row", "col"), P("col", None)),
        check_vma=False,
    )
```

profile of v0, /device:TPU:1, one launch (start us, length us, event | category | flops | bytes accessed | tf_op | source)
XLA Modules:
  0.0 175.2 jit_solution(6126663283762937878)
XLA Ops:
  7.2 0.0 copy-start
  7.2 2.5 %add_convert_fusion.b_ref = bf16[512,1664]{1,0:T(8,128)(2,1)S(1)} fusion(bf16[512,1664]{1,0:T(8,128)(2,1)} %param.4, bf16[512,1664]{1,0:T(8,128)(2,1)} %param.3), kind=kLoop, calls=%fused_computation.3 | loop fusion | flops 3407872 | bytes 5111808 | tf_op jit(solution)/shard_map/convert_element_type | solution.py:245
  9.7 0.0 copy-done
  9.7 0.0 copy-start.2
  9.7 1.1 fusion.2
  10.8 0.1 copy-done.2
  10.9 23.5 %all_to_all.25 = f32[16,32,512]{2,1,0:T(8,128)S(1)} all-to-all(f32[16,32,512]{2,1,0:T(8,128)S(1)} %bitcast.30), channel_id=1, replica_groups=mesh['row'=16,'col'=16] {'col'}, dimensions={0} | all-to-all | bytes 2097152 | tf_op jit(solution)/shard_map/all_to_all | solution.py:226
  34.4 0.1 reduce_sum.36
  34.4 1.1 broadcast_in_dim.13
  35.5 3.7 %all-to-all-start.1 = ((f32[16,32,512]{2,1,0:T(8,128)}), f32[16,32,512]{2,1,0:T(8,128)S(1)}, u32[]{:S(2)}, u32[]{:S(2)}) async-start(f32[16,32,512]{2,1,0:T(8,128)} %broadcast_in_dim.13), calls=%async_computation.1 | async-start | bytes 2097152 | tf_op jit(solution)/shard_map/all_to_all | solution.py:230
  39.2 15.0 %all-to-all-done.1 = f32[16,32,512]{2,1,0:T(8,128)S(1)} async-done(((f32[16,32,512]{2,1,0:T(8,128)}), f32[16,32,512]{2,1,0:T(8,128)S(1)}, u32[]{:S(2)}, u32[]{:S(2)}) %all-to-all-start.1) | async-done | bytes 1048608 | tf_op jit(solution)/shard_map/all_to_all | solution.py:230
  54.3 0.0 copy-start.3
  54.3 1.5 copy-done.3
  55.7 2.9 %shard_map.58 = f32[832,512]{1,0:T(8,128)} custom-call(s32[1]{0:T(128)} %bitcast.half_ref, bf16[512,1664]{1,0:T(8,128)(2,1)S(1)} %copy-done.3, f32[512,512]{1,0:T(8,128)S(1)} %bitcast.22), custom_call_target="tpu_custom_call" | custom-call | flops 2147483648 | bytes 4194304 | tf_op jit(solution)/shard_map/pallas_call | solution.py:213
  58.6 3.3 %collective-permute-start.2 = (f32[832,512]{1,0:T(8,128)}, f32[832,512]{1,0:T(8,128)}, u32[]{:S(2)}, u32[]{:S(2)}) collective-permute-start(f32[832,512]{1,0:T(8,128)} %shard_map.58), channel_id=1, source_target_pairs={{0,16},{16,0},{32,48},{48,32},{64,80},{80,64},{96,112},{112,96},{1... | collective-permute-start | bytes 5111816 | tf_op jit(solution)/shard_map/ppermute | solution.py:251
  61.9 1.6 shard_map.59
  63.5 0.1 collective-permute-start
  63.6 1.5 collective-permute-done
  65.2 0.7 broadcast_in_dim.14
  65.9 8.2 %all-to-all-start.2 = ((f32[8,40,128]{2,1,0:T(8,128)}), f32[8,40,128]{2,1,0:T(8,128)S(1)}, u32[]{:S(2)}, u32[]{:S(2)}) async-start(f32[8,40,128]{2,1,0:T(8,128)} %broadcast_in_dim.14), calls=%async_computation.2 | async-start | bytes 327680 | tf_op jit(solution)/shard_map/all_to_all | solution.py:230
  74.0 0.0 reduce-scatter.2.cloned.1.call-start
  74.1 0.0 collective-permute-done.2.refs_0_
  74.1 0.0 copy-start.4
  74.1 1.4 copy-done.4
  75.6 3.2 %shard_map.61 = f32[832,512]{1,0:T(8,128)S(1)} custom-call(s32[1]{0:T(128)} %bitcast.3.core_ref.half_ref, bf16[512,1664]{1,0:T(8,128)(2,1)S(1)} %copy-done.4, f32[512,512]{1,0:T(8,128)S(1)} %bitcast.24, f32[832,512]{1,0:T(8,128)} %collective-permute-done.2.refs_0_), custom_call_target="tpu_custom_call" | custom-call | flops 2147483648 | bytes 4194304 | tf_op jit(solution)/shard_map/pallas_call | solution.py:213
  78.8 0.0 copy-start.6
  78.8 1.2 copy-done.6
  80.0 0.0 reduce-scatter.2.cloned.1.call-update
  80.0 2.6 %all-to-all-done.2 = f32[8,40,128]{2,1,0:T(8,128)S(1)} async-done(((f32[8,40,128]{2,1,0:T(8,128)}), f32[8,40,128]{2,1,0:T(8,128)S(1)}, u32[]{:S(2)}, u32[]{:S(2)}) %all-to-all-start.2) | async-done | bytes 163872 | tf_op jit(solution)/shard_map/all_to_all | solution.py:230
  82.7 10.6 %all_to_all.26 = f32[16,40,128]{2,1,0:T(8,128)S(1)} all-to-all(f32[16,40,128]{2,1,0:T(8,128)S(1)} %broadcast_in_dim.15), channel_id=1, replica_groups=mesh['row'=16,'col'=16] {'col'}, dimensions={0} | all-to-all | bytes 655360 | tf_op jit(solution)/shard_map/all_to_all | solution.py:230
  93.3 3.5 %collective-permute-start.1 = (f32[5,128,128]{2,1,0:T(8,128)S(1)}, f32[5,128,128]{2,1,0:T(8,128)S(1)}, u32[]{:S(2)}, u32[]{:S(2)}) collective-permute-start(f32[5,128,128]{2,1,0:T(8,128)S(1)} %bitcast.26), channel_id=1, source_target_pairs={{0,16},{16,0},{32,48},{48,32},{64,80},{80,64},{96,112},{112,96},{1... | collective-permute-start | bytes 983048 | tf_op jit(solution)/shard_map/ppermute | solution.py:268
  96.9 1.3 collective-permute-done.1.theirs_ref
  98.1 18.3 %shard_map.60 = f32[512,512]{1,0:T(8,128)S(1)} custom-call(s32[1]{0:T(128)} %bitcast.3.core_ref.half_ref, f32[5,128,128]{2,1,0:T(8,128)S(1)} %bitcast.27, f32[5,128,128]{2,1,0:T(8,128)S(1)} %collective-permute-done.1.theirs_ref), custom_call_target="tpu_custom_call" | custom-call | flops 24999999488 | bytes 2097152 | tf_op jit(solution)/shard_map/pallas_call | solution.py:181
  116.4 0.0 copy-start.1
  116.4 1.0 copy-done.1
  117.4 1.9 %convolution_convert_fusion = bf16[512,512]{1,0:T(8,128)(2,1)S(1)} fusion(f32[512,512]{1,0:T(8,128)S(1)} %bitcast.25, f32[512,512]{1,0:T(8,128)S(1)} %shard_map.60), kind=kOutput, calls=%fused_computation.7 | convolution fusion | flops 1610874880 | bytes 2621440 | tf_op jit(solution)/shard_map/dot_general | solution.py:269
  119.3 0.0 reduce-scatter.2.cloned.1.call-done
  119.3 2.5 %convolution_convert_fusion.1 = bf16[104,512]{1,0:T(8,128)(2,1)S(1)} fusion(f32[104,512]{1,0:T(8,128)} %reduce-scatter.2.cloned.1.call-done, f32[512,512]{1,0:T(8,128)} %copy-done.1), kind=kOutput, calls=%fused_computation.8 | convolution fusion | flops 327208960 | bytes 1368064 | tf_op jit(solution)/shard_map/dot_general | solution.py:273
  121.8 21.0 %all_gather.3 = bf16[832,512]{1,0:T(8,128)(2,1)S(1)} all-gather(bf16[104,512]{1,0:T(8,128)(2,1)S(1)} %convolution_convert_fusion.1), channel_id=1, replica_groups={{0,32,64,96,128,160,192,224},{16,48,80,112,144,176,208,240},{1,33,65,97..., dimensions={0}, use_global_device_ids=true | all-gather | bytes 958464 | tf_op jit(solution)/shard_map/all_gather | solution.py:274
  142.8 5.7 %collective-permute-start.4 = (bf16[832,512]{1,0:T(8,128)(2,1)S(1)}, bf16[832,512]{1,0:T(8,128)(2,1)}, u32[]{:S(2)}, u32[]{:S(2)}) collective-permute-start(bf16[832,512]{1,0:T(8,128)(2,1)S(1)} %all_gather.3), channel_id=1, source_target_pairs={{0,16},{16,0},{32,48},{48,32},{64,80},{80,64},{96,112},{112,96},{1... | collective-permute-start | bytes 2555912 | tf_op jit(solution)/shard_map/ppermute | solution.py:242
  148.5 0.2 multiply_reduce_fusion
  148.7 0.1 collective-permute-start.3
  148.8 1.7 collective-permute-done.3
  150.5 0.6 broadcast_in_dim.16
  151.1 6.5 %all-to-all-start.4 = ((f32[16,4,128]{2,1,0:T(4,128)}), f32[16,4,128]{2,1,0:T(4,128)S(1)}, u32[]{:S(2)}, u32[]{:S(2)}) async-start(f32[16,4,128]{2,1,0:T(4,128)} %broadcast_in_dim.16), calls=%async_computation.5 | async-start | bytes 65536 | tf_op jit(solution)/shard_map/all_to_all | solution.py:230
  157.6 0.0 copy-start.5
  157.6 0.0 collective-permute-done.4
  157.6 1.4 broadcast_select_fusion.1
  159.0 0.0 copy-start.8
  159.0 0.0 copy-start.9
  159.0 0.9 copy-done.8
  160.0 0.2 copy-done.9
  160.2 0.0 copy-done.5
  160.2 2.4 %subtract_convert_fusion = bf16[512,1664]{1,0:T(8,128)(2,1)} fusion(bf16[512,1664]{1,0:T(8,128)(2,1)S(1)} %copy-done.5, bf16[512,512]{1,0:T(8,128)(2,1)S(1)} %convolution_convert_fusion, bf16[832,512]{1,0:T(8,128)(2,1)S(1)} %get-tuple-element.16, bf16[832,512]{1,0:T(8,128)(2,1)S(1)} %get-tuple-element.15), kind=kOutput, calls=%fused_computation.2 | convolution fusion | flops 879230976 | bytes 5636096 | tf_op jit(solution)/shard_map/dot_general | solution.py:281
  162.6 1.4 all-to-all-done.4
  164.1 1.9 %convert_multiply_fusion = f32[1664,512]{1,0:T(8,128)S(1)} fusion(f32[512]{0:T(512)S(1)} %rsqrt_bitcast_fusion, bf16[832,512]{1,0:T(8,128)(2,1)} %copy-done.9, bf16[832,512]{1,0:T(8,128)(2,1)} %copy-done.8), kind=kLoop, calls=%fused_computation.1 | loop fusion | flops 4259840 | bytes 5113856 | tf_op jit(solution)/shard_map/mul | solution.py:287
  166.0 0.0 copy-start.7
  166.0 2.3 %multiply_convert_fusion = bf16[512,1664]{1,0:T(8,128)(2,1)} fusion(bf16[512,512]{1,0:T(8,128)(2,1)S(1)} %convolution_convert_fusion, f32[1664,512]{1,0:T(8,128)S(1)} %convert_multiply_fusion), kind=kOutput, calls=%fused_computation | convolution fusion | flops 874971136 | bytes 5636096 | tf_op jit(solution)/shard_map/dot_general | solution.py:289
  168.3 0.0 copy-done.7
  (7 shorter events, 0.1 us)
Async XLA Ops:
  7.2 2.5 %copy-start = (bf16[1664,512]{1,0:T(8,128)(2,1)S(1)}, bf16[1664,512]{1,0:T(8,128)(2,1)}, u32[]{:S(2)}) copy-start(bf16[1664,512]{1,0:T(8,128)(2,1)} %param.5) | copy-start | bytes 5111812
  9.7 1.2 copy-start.2
  35.5 18.7 %all-to-all-start.1 = ((f32[16,32,512]{2,1,0:T(8,128)}), f32[16,32,512]{2,1,0:T(8,128)S(1)}, u32[]{:S(2)}, u32[]{:S(2)}) async-start(f32[16,32,512]{2,1,0:T(8,128)} %broadcast_in_dim.13), calls=%async_computation.1 | async-start | bytes 2097152 | tf_op jit(solution)/shard_map/all_to_all | solution.py:230
  54.3 1.5 copy-start.3
  58.6 15.5 %collective-permute-start.2 = (f32[832,512]{1,0:T(8,128)}, f32[832,512]{1,0:T(8,128)}, u32[]{:S(2)}, u32[]{:S(2)}) collective-permute-start(f32[832,512]{1,0:T(8,128)} %shard_map.58), channel_id=1, source_target_pairs={{0,16},{16,0},{32,48},{48,32},{64,80},{80,64},{96,112},{112,96},{1... | collective-permute-start | bytes 5111816 | tf_op jit(solution)/shard_map/ppermute | solution.py:251
  63.5 1.6 collective-permute-start
  65.9 16.8 %all-to-all-start.2 = ((f32[8,40,128]{2,1,0:T(8,128)}), f32[8,40,128]{2,1,0:T(8,128)S(1)}, u32[]{:S(2)}, u32[]{:S(2)}) async-start(f32[8,40,128]{2,1,0:T(8,128)} %broadcast_in_dim.14), calls=%async_computation.2 | async-start | bytes 327680 | tf_op jit(solution)/shard_map/all_to_all | solution.py:230
  74.0 45.3 %reduce-scatter.2.cloned.1.call-start = ((), (), s32[]{:S(2)}) async-start(), calls=%async_computation.6 | async-start | bytes 1916928 | tf_op jit(solution)/shard_map/reduce_scatter | solution.py:262
  74.1 1.5 copy-start.4
  78.8 1.2 copy-start.6
  93.3 4.8 %collective-permute-start.1 = (f32[5,128,128]{2,1,0:T(8,128)S(1)}, f32[5,128,128]{2,1,0:T(8,128)S(1)}, u32[]{:S(2)}, u32[]{:S(2)}) collective-permute-start(f32[5,128,128]{2,1,0:T(8,128)S(1)} %bitcast.26), channel_id=1, source_target_pairs={{0,16},{16,0},{32,48},{48,32},{64,80},{80,64},{96,112},{112,96},{1... | collective-permute-start | bytes 983048 | tf_op jit(solution)/shard_map/ppermute | solution.py:268
  116.4 1.0 copy-start.1
  142.8 14.8 %collective-permute-start.4 = (bf16[832,512]{1,0:T(8,128)(2,1)S(1)}, bf16[832,512]{1,0:T(8,128)(2,1)}, u32[]{:S(2)}, u32[]{:S(2)}) collective-permute-start(bf16[832,512]{1,0:T(8,128)(2,1)S(1)} %all_gather.3), channel_id=1, source_target_pairs={{0,16},{16,0},{32,48},{48,32},{64,80},{80,64},{96,112},{112,96},{1... | collective-permute-start | bytes 2555912 | tf_op jit(solution)/shard_map/ppermute | solution.py:242
  148.7 1.8 %collective-permute-start.3 = (f32[4,128]{1,0:T(4,128)S(1)}, f32[4,128]{1,0:T(4,128)S(1)}, u32[]{:S(2)}, u32[]{:S(2)}) collective-permute-start(f32[4,128]{1,0:T(4,128)S(1)} %bitcast.31), channel_id=1, source_target_pairs={{0,16},{16,0},{32,48},{48,32},{64,80},{80,64},{96,112},{112,96},{1... | collective-permute-start | bytes 6152 | tf_op jit(solution)/shard_map/ppermute | solution.py:278
  151.1 13.0 %all-to-all-start.4 = ((f32[16,4,128]{2,1,0:T(4,128)}), f32[16,4,128]{2,1,0:T(4,128)S(1)}, u32[]{:S(2)}, u32[]{:S(2)}) async-start(f32[16,4,128]{2,1,0:T(4,128)} %broadcast_in_dim.16), calls=%async_computation.5 | async-start | bytes 65536 | tf_op jit(solution)/shard_map/all_to_all | solution.py:230
  157.6 2.6 %copy-start.5 = (bf16[512,1664]{1,0:T(8,128)(2,1)S(1)}, bf16[512,1664]{1,0:T(8,128)(2,1)}, u32[]{:S(2)}) copy-start(bf16[512,1664]{1,0:T(8,128)(2,1)} %copy-done.2) | copy-start | bytes 5111812
  159.0 0.9 copy-start.8
  159.0 1.2 copy-start.9
  166.0 2.4 %copy-start.7 = (f32[1664,512]{1,0:T(8,128)}, f32[1664,512]{1,0:T(8,128)S(1)}, u32[]{:S(2)}) copy-start(f32[1664,512]{1,0:T(8,128)S(1)} %convert_multiply_fusion) | copy-start | bytes 10223620
Sparse Core Ops, SparseCore 0:
  80.1 34.6 reduce-scatter.1
where the time goes:
time: 176 us; the launch traced here: 175 us
  blocking collectives  55.1 us (31%)
  starting transfers between devices  31.1 us (18%)
  Pallas kernels  26.1 us (15%)
  waiting for transfers between devices  23.6 us (13%)
  between operations  14.3 us (8%)
  matrix products  10.2 us (6%)
  local copies, waits for them, and re-layouts  8.72 us (5%)
  other arithmetic  6.13 us (3%)
    all_to_all x1, blocking collectives, scatter_sum(): return jnp.sum(lax.all_to_all(parts, axis, 0, 0), axis=0)  23.5 us
    all_gather x1, blocking collectives, local(): lax.all_gather(back_rows.astype(jnp.bfloat16), 'row', axis_index_groups=a...  21 us
    all_to_all x3, waiting for transfers between devices, exchange(): lax.all_to_all(jnp.broadcast_to(x, (size,) + x.shape), axis, 0, 0, axis_i...  19.1 us
    all_to_all x3, starting transfers between devices, exchange(): lax.all_to_all(jnp.broadcast_to(x, (size,) + x.shape), axis, 0, 0, axis_i...  18.4 us
    pallas_call x1, Pallas kernels, inverse_factor(): pl.pallas_call(inverse_factor_kernel, out_shape=jax.ShapeDtypeStruct((RAN...  18.3 us
    all_to_all x1, blocking collectives, exchange(): lax.all_to_all(jnp.broadcast_to(x, (size,) + x.shape), axis, 0, 0, axis_i...  10.6 us
    unnamed x20, local copies, waits for them, and re-layouts  6.29 us
    pallas_call x2, Pallas kernels, weights_half(): pl.pallas_call(weights_kernel, out_shape=jax.ShapeDtypeStruct((rows, RANK...  6.15 us
  transfers between devices with their start and end apart: 9, of which 6 were waited for; matrix products, arithmetic and copies ran while one was open for 4% of the time, Pallas kernels for 13%

commit v1 on v0

--- a/solution.py
+++ b/solution.py
@@ -199,9 +199,12 @@
     start = b_ref.shape[1] - w_ref.shape[0]
     half = half_ref[0]
     rows = b_ref[:, pl.ds(pl.multiple_of(half * start, BLOCK), w_ref.shape[0])]
-    for n, piece in enumerate(pieces(p_ref[...])):
-        term = lax.dot_general(rows, piece, (((0,), (0,)), ((), ())), preferred_element_type=jnp.float32)
-        w_ref[...] = term if n == 0 else w_ref[...] + term
+    w_ref[...] = lax.dot_general(
+        jnp.concatenate([rows] * 3, axis=0),
+        jnp.concatenate(pieces(p_ref[...]), axis=0),
+        (((0,), (0,)), ((), ())),
+        preferred_element_type=jnp.float32,
+    )
     own = w_ref[pl.ds(pl.multiple_of(half * (o_ref.shape[0] - start), SUB), o_ref.shape[0]), :]
     o_ref[...] = own + added[0][...] if added else own
 
@@ -221,6 +224,59 @@
     )(half.astype(jnp.int32).reshape(1), blended, projected, *added)
 
 
+def finish_kernel(scale_ref, left_ref, right_hbm, factor_hbm, update_hbm, right_ref, factor_ref, update_ref, sems):
+    total = right_ref.shape[0]
+    cut = (total // BLOCK + 1) // 2 * BLOCK
+    chunks = (slice(0, cut), slice(cut, total))
+    arrivals = [
+        pltpu.make_async_copy(right_hbm.at[chunk, :], right_ref.at[chunk, :], sems.at[n])
+        for n, chunk in enumerate(chunks)
+    ]
+    for copy in arrivals:
+        copy.start()
+    leaving = []
+    for n, chunk in enumerate(chunks):
+        arrivals[n].wait()
+        factor_ref[chunk, :] = right_ref[chunk, :].astype(jnp.float32) * scale_ref[...]
+        leaving.append(
+            pltpu.make_async_copy(factor_ref.at[chunk, :], factor_hbm.at[chunk, :], sems.at[2 + n])
+        )
+        leaving[-1].start()
+        update = lax.dot_general(
+            left_ref[...],
+            factor_ref[chunk, :].astype(jnp.bfloat16),
+            (((1,), (1,)), ((), ())),
+            preferred_element_type=jnp.float32,
+        )
+        update_ref[:, chunk] = (update * math.sqrt(ROWS / RANK)).astype(jnp.bfloat16)
+        leaving.append(
+            pltpu.make_async_copy(update_ref.at[:, chunk], update_hbm.at[:, chunk], sems.at[4 + n])
+        )
+        leaving[-1].start()
+    for copy in leaving:
+        copy.wait()
+
+
+def finish(scale, left_bf, right_bf):
+    factor = jax.ShapeDtypeStruct(right_bf.shape, jnp.float32)
+    update = jax.ShapeDtypeStruct((left_bf.shape[0], right_bf.shape[0]), jnp.bfloat16)
+    vmem, hbm = pl.BlockSpec(memory_space=pltpu.VMEM), pl.BlockSpec(memory_space=pl.ANY)
+    return pl.pallas_call(
+        finish_kernel,
+        out_shape=(factor, update),
+        in_specs=[vmem, vmem, hbm],
+        out_specs=(hbm, hbm),
+        scratch_shapes=[
+            pltpu.VMEM(right_bf.shape, right_bf.dtype),
+            pltpu.VMEM(factor.shape, factor.dtype),
+            pltpu.VMEM(update.shape, update.dtype),
+            pltpu.SemaphoreType.DMA((6,)),
+        ],
+        compiler_params=pltpu.CompilerParams(vmem_limit_bytes=56 * 1024 * 1024),
+        cost_estimate=pl.CostEstimate(flops=2**30, bytes_accessed=2**23, transcendentals=0),
+    )(scale, left_bf, right_bf)
+
+
 def scatter_sum(x, axis, size):
     parts = x.reshape((size, x.shape[0] // size) + x.shape[1:])
     return jnp.sum(lax.all_to_all(parts, axis, 0, 0), axis=0)
@@ -284,12 +340,8 @@
     new_momentum = (blended.astype(jnp.float32) - FEEDBACK * correction).astype(jnp.bfloat16)
     squares, new_momentum = lax.optimization_barrier((squares, new_momentum))
     back_squares = jnp.sum(squares, axis=0).reshape(RANK)
-    new_factor = right_bf.astype(jnp.float32) * (1.0 / jnp.sqrt(back_squares / COLS + NORM_EPS))
-    factor_bf = new_factor.astype(jnp.bfloat16)
-    update_full = lax.dot_general(
-        left_bf, factor_bf, (((1,), (1,)), ((), ())), preferred_element_type=jnp.float32
-    )
-    weight_update = (update_full * math.sqrt(ROWS / RANK)).astype(jnp.bfloat16)
+    scale = (1.0 / jnp.sqrt(back_squares / COLS + NORM_EPS)).reshape(1, RANK)
+    new_factor, weight_update = finish(scale, left_bf, right_bf)
     return (new_momentum, weight_update, new_factor)
 
 

time: 176 us -> 177 us (level)
  Pallas kernels: 26.1 us -> 31.2 us
  matrix products: 10.2 us -> 8 us
    pallas_call x0 -> x1, Pallas kernels: none -> 5.13 us  [finish(): pl.pallas_call(finish_kernel, out_shape=(factor, update), in_specs=[vmem,...]
    dot_general x1 -> x0, matrix products: 2.34 us -> none  [local(): lax.dot_general(left_bf, factor_bf, (((1,), (1,)), ((), ())), preferred_e...]
    mul x1 -> x0, other arithmetic: 1.89 us -> none  [local(): right_bf.astype(jnp.float32)]
    unnamed x20 -> x16, local copies, waits for them, and re-layouts: 6.29 us -> 5.4 us
  transfers between devices with their start and end apart: 9 -> 9, of which waited for: 6 -> 6; matrix products, arithmetic and copies ran while one was open for 4% -> 5% of each run, Pallas kernels for 13% -> 13%
where the time goes in v1:
time: 177 us
  blocking collectives  55.2 us (31%)
  Pallas kernels  31.2 us (18%)
  starting transfers between devices  31 us (18%)
  waiting for transfers between devices  23.2 us (13%)
  between operations  14.3 us (8%)
  matrix products  8 us (5%)
  local copies, waits for them, and re-layouts  7.84 us (4%)
  other arithmetic  6.16 us (3%)
    all_to_all x1, blocking collectives, scatter_sum(): return jnp.sum(lax.all_to_all(parts, axis, 0, 0), axis=0)  23.5 us
    all_gather x1, blocking collectives, local(): lax.all_gather(back_rows.astype(jnp.bfloat16), 'row', axis_index_groups=a...  21.1 us
    all_to_all x3, waiting for transfers between devices, exchange(): lax.all_to_all(jnp.broadcast_to(x, (size,) + x.shape), axis, 0, 0, axis_i...  18.7 us
    all_to_all x3, starting transfers between devices, exchange(): lax.all_to_all(jnp.broadcast_to(x, (size,) + x.shape), axis, 0, 0, axis_i...  18.4 us
    pallas_call x1, Pallas kernels, inverse_factor(): pl.pallas_call(inverse_factor_kernel, out_shape=jax.ShapeDtypeStruct((RAN...  18.3 us
    all_to_all x1, blocking collectives, exchange(): lax.all_to_all(jnp.broadcast_to(x, (size,) + x.shape), axis, 0, 0, axis_i...  10.6 us
    pallas_call x2, Pallas kernels, weights_half(): pl.pallas_call(weights_kernel, out_shape=jax.ShapeDtypeStruct((rows, RANK...  6.15 us
    ppermute x1, starting transfers between devices, both_halves(): theirs = lax.ppermute(mine, 'row', other)  5.58 us
  transfers between devices with their start and end apart: 9, of which 6 were waited for; matrix products, arithmetic and copies ran while one was open for 5% of the time, Pallas kernels for 13%

profile of v1, /device:TPU:1, one launch (start us, length us, event | category | flops | bytes accessed | tf_op | source)
XLA Modules:
  0.0 176.9 jit_solution(7092164784889200264)
XLA Ops:
  7.2 0.0 copy-start
  7.2 2.5 %add_convert_fusion.b_ref = bf16[512,1664]{1,0:T(8,128)(2,1)S(1)} fusion(bf16[512,1664]{1,0:T(8,128)(2,1)} %param.4, bf16[512,1664]{1,0:T(8,128)(2,1)} %param.3), kind=kLoop, calls=%fused_computation.1 | loop fusion | flops 3407872 | bytes 5111808 | tf_op jit(solution)/shard_map/convert_element_type | solution.py:301
  9.7 0.0 copy-done
  9.7 0.0 copy-start.2
  9.7 1.1 fusion
  10.8 0.1 copy-done.2
  10.9 23.5 %all_to_all.25 = f32[16,32,512]{2,1,0:T(8,128)S(1)} all-to-all(f32[16,32,512]{2,1,0:T(8,128)S(1)} %bitcast.28), channel_id=1, replica_groups=mesh['row'=16,'col'=16] {'col'}, dimensions={0} | all-to-all | bytes 2097152 | tf_op jit(solution)/shard_map/all_to_all | solution.py:282
  34.4 0.1 reduce_sum.36
  34.4 1.1 broadcast_in_dim.12
  35.5 3.7 %all-to-all-start.1 = ((f32[16,32,512]{2,1,0:T(8,128)}), f32[16,32,512]{2,1,0:T(8,128)S(1)}, u32[]{:S(2)}, u32[]{:S(2)}) async-start(f32[16,32,512]{2,1,0:T(8,128)} %broadcast_in_dim.12), calls=%async_computation.1 | async-start | bytes 2097152 | tf_op jit(solution)/shard_map/all_to_all | solution.py:286
  39.2 15.0 %all-to-all-done.1 = f32[16,32,512]{2,1,0:T(8,128)S(1)} async-done(((f32[16,32,512]{2,1,0:T(8,128)}), f32[16,32,512]{2,1,0:T(8,128)S(1)}, u32[]{:S(2)}, u32[]{:S(2)}) %all-to-all-start.1) | async-done | bytes 1048608 | tf_op jit(solution)/shard_map/all_to_all | solution.py:286
  54.3 0.0 copy-start.3
  54.3 1.5 copy-done.3
  55.7 2.9 %shard_map.58 = f32[832,512]{1,0:T(8,128)} custom-call(s32[1]{0:T(128)} %bitcast.half_ref, bf16[512,1664]{1,0:T(8,128)(2,1)S(1)} %copy-done.3, f32[512,512]{1,0:T(8,128)S(1)} %bitcast.20), custom_call_target="tpu_custom_call" | custom-call | flops 2147483648 | bytes 4194304 | tf_op jit(solution)/shard_map/pallas_call | solution.py:216
  58.6 3.3 %collective-permute-start.2 = (f32[832,512]{1,0:T(8,128)}, f32[832,512]{1,0:T(8,128)}, u32[]{:S(2)}, u32[]{:S(2)}) collective-permute-start(f32[832,512]{1,0:T(8,128)} %shard_map.58), channel_id=1, source_target_pairs={{0,16},{16,0},{32,48},{48,32},{64,80},{80,64},{96,112},{112,96},{1... | collective-permute-start | bytes 5111816 | tf_op jit(solution)/shard_map/ppermute | solution.py:307
  61.9 1.6 shard_map.59
  63.5 0.1 collective-permute-start
  63.6 1.5 collective-permute-done
  65.2 0.7 broadcast_in_dim.13
  65.9 8.2 %all-to-all-start.2 = ((f32[8,40,128]{2,1,0:T(8,128)}), f32[8,40,128]{2,1,0:T(8,128)S(1)}, u32[]{:S(2)}, u32[]{:S(2)}) async-start(f32[8,40,128]{2,1,0:T(8,128)} %broadcast_in_dim.13), calls=%async_computation.2 | async-start | bytes 327680 | tf_op jit(solution)/shard_map/all_to_all | solution.py:286
  74.0 0.0 reduce-scatter.2.cloned.1.call-start
  74.1 0.0 collective-permute-done.2.refs_0_
  74.1 0.0 copy-start.4
  74.1 1.4 copy-done.4
  75.6 3.2 %shard_map.61 = f32[832,512]{1,0:T(8,128)S(1)} custom-call(s32[1]{0:T(128)} %bitcast.3.core_ref.half_ref, bf16[512,1664]{1,0:T(8,128)(2,1)S(1)} %copy-done.4, f32[512,512]{1,0:T(8,128)S(1)} %bitcast.22, f32[832,512]{1,0:T(8,128)} %collective-permute-done.2.refs_0_), custom_call_target="tpu_custom_call" | custom-call | flops 2147483648 | bytes 4194304 | tf_op jit(solution)/shard_map/pallas_call | solution.py:216
  78.8 0.0 copy-start.6
  78.8 1.2 copy-done.6
  80.0 0.0 reduce-scatter.2.cloned.1.call-update
  80.0 2.6 %all-to-all-done.2 = f32[8,40,128]{2,1,0:T(8,128)S(1)} async-done(((f32[8,40,128]{2,1,0:T(8,128)}), f32[8,40,128]{2,1,0:T(8,128)S(1)}, u32[]{:S(2)}, u32[]{:S(2)}) %all-to-all-start.2) | async-done | bytes 163872 | tf_op jit(solution)/shard_map/all_to_all | solution.py:286
  82.7 10.6 %all_to_all.26 = f32[16,40,128]{2,1,0:T(8,128)S(1)} all-to-all(f32[16,40,128]{2,1,0:T(8,128)S(1)} %broadcast_in_dim.14), channel_id=1, replica_groups=mesh['row'=16,'col'=16] {'col'}, dimensions={0} | all-to-all | bytes 655360 | tf_op jit(solution)/shard_map/all_to_all | solution.py:286
  93.3 3.5 %collective-permute-start.1 = (f32[5,128,128]{2,1,0:T(8,128)S(1)}, f32[5,128,128]{2,1,0:T(8,128)S(1)}, u32[]{:S(2)}, u32[]{:S(2)}) collective-permute-start(f32[5,128,128]{2,1,0:T(8,128)S(1)} %bitcast.24), channel_id=1, source_target_pairs={{0,16},{16,0},{32,48},{48,32},{64,80},{80,64},{96,112},{112,96},{1... | collective-permute-start | bytes 983048 | tf_op jit(solution)/shard_map/ppermute | solution.py:324
  96.9 1.3 collective-permute-done.1.theirs_ref
  98.1 18.3 %shard_map.60 = f32[512,512]{1,0:T(8,128)S(1)} custom-call(s32[1]{0:T(128)} %bitcast.3.core_ref.half_ref, f32[5,128,128]{2,1,0:T(8,128)S(1)} %bitcast.25, f32[5,128,128]{2,1,0:T(8,128)S(1)} %collective-permute-done.1.theirs_ref), custom_call_target="tpu_custom_call" | custom-call | flops 24999999488 | bytes 2097152 | tf_op jit(solution)/shard_map/pallas_call | solution.py:181
  116.4 0.0 copy-start.1
  116.4 1.0 copy-done.1
  117.4 1.9 %convolution_convert_fusion.left_ref = bf16[512,512]{1,0:T(8,128)(2,1)S(1)} fusion(f32[512,512]{1,0:T(8,128)S(1)} %bitcast.23, f32[512,512]{1,0:T(8,128)S(1)} %shard_map.60), kind=kOutput, calls=%fused_computation.4 | convolution fusion | flops 1610874880 | bytes 2621440 | tf_op jit(solution)/shard_map/dot_general | solution.py:325
  119.3 0.0 copy-start.7
  119.3 0.0 reduce-scatter.2.cloned.1.call-done
  119.3 2.6 %convolution_convert_fusion.1 = bf16[104,512]{1,0:T(8,128)(2,1)S(1)} fusion(f32[104,512]{1,0:T(8,128)} %reduce-scatter.2.cloned.1.call-done, f32[512,512]{1,0:T(8,128)} %copy-done.1), kind=kOutput, calls=%fused_computation.5 | convolution fusion | flops 327208960 | bytes 1368064 | tf_op jit(solution)/shard_map/dot_general | solution.py:329
  121.9 21.1 %all_gather.3 = bf16[832,512]{1,0:T(8,128)(2,1)S(1)} all-gather(bf16[104,512]{1,0:T(8,128)(2,1)S(1)} %convolution_convert_fusion.1), channel_id=1, replica_groups={{0,32,64,96,128,160,192,224},{16,48,80,112,144,176,208,240},{1,33,65,97..., dimensions={0}, use_global_device_ids=true | all-gather | bytes 958464 | tf_op jit(solution)/shard_map/all_gather | solution.py:330
  143.0 5.6 %collective-permute-start.4 = (bf16[832,512]{1,0:T(8,128)(2,1)S(1)}, bf16[832,512]{1,0:T(8,128)(2,1)}, u32[]{:S(2)}, u32[]{:S(2)}) collective-permute-start(bf16[832,512]{1,0:T(8,128)(2,1)S(1)} %all_gather.3), channel_id=1, source_target_pairs={{0,16},{16,0},{32,48},{48,32},{64,80},{80,64},{96,112},{112,96},{1... | collective-permute-start | bytes 2555912 | tf_op jit(solution)/shard_map/ppermute | solution.py:298
  148.6 0.2 multiply_reduce_fusion
  148.8 0.1 collective-permute-start.3
  148.9 1.7 collective-permute-done.3
  150.6 0.6 broadcast_in_dim.15
  151.2 6.5 %all-to-all-start.4 = ((f32[16,4,128]{2,1,0:T(4,128)}), f32[16,4,128]{2,1,0:T(4,128)S(1)}, u32[]{:S(2)}, u32[]{:S(2)}) async-start(f32[16,4,128]{2,1,0:T(4,128)} %broadcast_in_dim.15), calls=%async_computation.5 | async-start | bytes 65536 | tf_op jit(solution)/shard_map/all_to_all | solution.py:286
  157.8 0.0 copy-start.5
  157.8 0.0 collective-permute-done.4
  157.8 1.4 broadcast_select_fusion.1
  159.2 0.0 copy-done.7
  159.2 0.3 copy-done.5
  159.5 2.4 %subtract_convert_fusion = bf16[512,1664]{1,0:T(8,128)(2,1)} fusion(bf16[512,1664]{1,0:T(8,128)(2,1)S(1)} %copy-done.5, bf16[512,512]{1,0:T(8,128)(2,1)S(1)} %convolution_convert_fusion.left_ref, bf16[832,512]{1,0:T(8,128)(2,1)S(1)} %get-tuple-element.20, bf16[832,512]{1,0:T(8,128)(2,1)S(1)} %get-tuple-element.19), kind=kOutput, calls=%fused_computation | convolution fusion | flops 879230976 | bytes 5636096 | tf_op jit(solution)/shard_map/dot_general | solution.py:337
  161.9 1.3 pad_maximum_fusion.right_hbm
  163.2 1.0 all-to-all-done.4
  164.3 0.6 add_rsqrt_fusion
  164.9 5.1 %shard_map.62 = (f32[1664,512]{1,0:T(8,128)}, bf16[512,1664]{1,0:T(8,128)(2,1)}) custom-call(f32[1,512]{1,0:T(1,128)} %bitcast.30, bf16[512,512]{1,0:T(8,128)(2,1)} %copy-done.7, bf16[1664,512]{1,0:T(8,128)(2,1)} %pad_maximum_fusion.right_hbm), custom_call_target="tpu_custom_call" | custom-call | flops 1073741824 | bytes 8388608 | tf_op jit(solution)/shard_map/pallas_call | solution.py:264
  (6 shorter events, 0.1 us)
Async XLA Ops:
  7.2 2.5 %copy-start = (bf16[1664,512]{1,0:T(8,128)(2,1)S(1)}, bf16[1664,512]{1,0:T(8,128)(2,1)}, u32[]{:S(2)}) copy-start(bf16[1664,512]{1,0:T(8,128)(2,1)} %param.5) | copy-start | bytes 5111812
  9.7 1.2 copy-start.2
  35.5 18.7 %all-to-all-start.1 = ((f32[16,32,512]{2,1,0:T(8,128)}), f32[16,32,512]{2,1,0:T(8,128)S(1)}, u32[]{:S(2)}, u32[]{:S(2)}) async-start(f32[16,32,512]{2,1,0:T(8,128)} %broadcast_in_dim.12), calls=%async_computation.1 | async-start | bytes 2097152 | tf_op jit(solution)/shard_map/all_to_all | solution.py:286
  54.3 1.5 copy-start.3
  58.6 15.5 %collective-permute-start.2 = (f32[832,512]{1,0:T(8,128)}, f32[832,512]{1,0:T(8,128)}, u32[]{:S(2)}, u32[]{:S(2)}) collective-permute-start(f32[832,512]{1,0:T(8,128)} %shard_map.58), channel_id=1, source_target_pairs={{0,16},{16,0},{32,48},{48,32},{64,80},{80,64},{96,112},{112,96},{1... | collective-permute-start | bytes 5111816 | tf_op jit(solution)/shard_map/ppermute | solution.py:307
  63.5 1.6 collective-permute-start
  65.9 16.8 %all-to-all-start.2 = ((f32[8,40,128]{2,1,0:T(8,128)}), f32[8,40,128]{2,1,0:T(8,128)S(1)}, u32[]{:S(2)}, u32[]{:S(2)}) async-start(f32[8,40,128]{2,1,0:T(8,128)} %broadcast_in_dim.13), calls=%async_computation.2 | async-start | bytes 327680 | tf_op jit(solution)/shard_map/all_to_all | solution.py:286
  74.0 45.3 %reduce-scatter.2.cloned.1.call-start = ((), (), s32[]{:S(2)}) async-start(), calls=%async_computation.6 | async-start | bytes 1916928 | tf_op jit(solution)/shard_map/reduce_scatter | solution.py:318
  74.1 1.5 copy-start.4
  78.8 1.2 copy-start.6
  93.3 4.8 %collective-permute-start.1 = (f32[5,128,128]{2,1,0:T(8,128)S(1)}, f32[5,128,128]{2,1,0:T(8,128)S(1)}, u32[]{:S(2)}, u32[]{:S(2)}) collective-permute-start(f32[5,128,128]{2,1,0:T(8,128)S(1)} %bitcast.24), channel_id=1, source_target_pairs={{0,16},{16,0},{32,48},{48,32},{64,80},{80,64},{96,112},{112,96},{1... | collective-permute-start | bytes 983048 | tf_op jit(solution)/shard_map/ppermute | solution.py:324
  116.4 1.0 copy-start.1
  119.3 39.9 %copy-start.7 = (bf16[512,512]{1,0:T(8,128)(2,1)}, bf16[512,512]{1,0:T(8,128)(2,1)S(1)}, u32[]{:S(2)}) copy-start(bf16[512,512]{1,0:T(8,128)(2,1)S(1)} %convolution_convert_fusion.left_ref) | copy-start | bytes 1572868
  143.0 14.8 %collective-permute-start.4 = (bf16[832,512]{1,0:T(8,128)(2,1)S(1)}, bf16[832,512]{1,0:T(8,128)(2,1)}, u32[]{:S(2)}, u32[]{:S(2)}) collective-permute-start(bf16[832,512]{1,0:T(8,128)(2,1)S(1)} %all_gather.3), channel_id=1, source_target_pairs={{0,16},{16,0},{32,48},{48,32},{64,80},{80,64},{96,112},{112,96},{1... | collective-permute-start | bytes 2555912 | tf_op jit(solution)/shard_map/ppermute | solution.py:298
  148.8 1.8 %collective-permute-start.3 = (f32[4,128]{1,0:T(4,128)S(1)}, f32[4,128]{1,0:T(4,128)S(1)}, u32[]{:S(2)}, u32[]{:S(2)}) collective-permute-start(f32[4,128]{1,0:T(4,128)S(1)} %bitcast.29), channel_id=1, source_target_pairs={{0,16},{16,0},{32,48},{48,32},{64,80},{80,64},{96,112},{112,96},{1... | collective-permute-start | bytes 6152 | tf_op jit(solution)/shard_map/ppermute | solution.py:334
  151.2 13.0 %all-to-all-start.4 = ((f32[16,4,128]{2,1,0:T(4,128)}), f32[16,4,128]{2,1,0:T(4,128)S(1)}, u32[]{:S(2)}, u32[]{:S(2)}) async-start(f32[16,4,128]{2,1,0:T(4,128)} %broadcast_in_dim.15), calls=%async_computation.5 | async-start | bytes 65536 | tf_op jit(solution)/shard_map/all_to_all | solution.py:286
  157.8 1.7 copy-start.5
Sparse Core Ops, SparseCore 0:
  80.1 34.6 reduce-scatter.1

commit v2 on v0

--- a/solution.py
+++ b/solution.py
@@ -262,7 +262,10 @@
     weights = lax.psum_scatter(
         weights, "row", scatter_dimension=0, axis_index_groups=along_z, tiled=True
     )
-    packed = jnp.sum(exchange(packed, "row", along_z, n_z), axis=0)
+    step = 1
+    while step < n_z:
+        packed = packed + lax.ppermute(packed, "row", [(i, i ^ (2 * step)) for i in range(n_row)])
+        step *= 2
     packed = exchange(packed, "col", None, n_col).reshape(len(PAIRS) // 2, BLOCK, BLOCK)
 
     inverse = inverse_factor(core, packed, lax.ppermute(packed, "row", other))

time: 176 us -> 178 us (1.011)
  blocking collectives: 55.1 us -> 57.7 us
  local copies, waits for them, and re-layouts: 8.72 us -> 6.61 us
    all_to_all x3 -> x2, starting transfers between devices: 18.4 us -> 7.13 us  [exchange(): lax.all_to_all(jnp.broadcast_to(x, (size,) + x.shape), axis, 0, 0, axis_i...]
    ppermute x0 -> x3, starting transfers between devices: none -> 10.8 us  [local(): lax.ppermute(packed, 'row', [(i, i ^ 2 * step) for i in range(n_row)])]
    ppermute x0 -> x3, waiting for transfers between devices: none -> 3.54 us  [local(): lax.ppermute(packed, 'row', [(i, i ^ 2 * step) for i in range(n_row)])]
    all_to_all x3 -> x2, waiting for transfers between devices: 19.1 us -> 16.4 us  [exchange(): lax.all_to_all(jnp.broadcast_to(x, (size,) + x.shape), axis, 0, 0, axis_i...]
    all_gather x1, blocking collectives: 21 us -> 23.6 us  [local(): lax.all_gather(back_rows.astype(jnp.bfloat16), 'row', axis_index_groups=a...]
    ppermute x1, waiting for transfers between devices: 0.01 us -> 1.84 us  [local(): theirs = lax.ppermute(theirs, 'row', other)]
  transfers between devices with their start and end apart: 9 -> 11, of which waited for: 6 -> 8; matrix products, arithmetic and copies ran while one was open for 4% -> 4% of each run, Pallas kernels for 13% -> 13%
where the time goes in v2:
time: 178 us
  blocking collectives  57.7 us (32%)
  starting transfers between devices  32.1 us (18%)
  Pallas kernels  26.1 us (15%)
  waiting for transfers between devices  24.7 us (14%)
  between operations  14.3 us (8%)
  matrix products  10.2 us (6%)
  local copies, waits for them, and re-layouts  6.61 us (4%)
  other arithmetic  6.14 us (3%)
    all_gather x1, blocking collectives, local(): lax.all_gather(back_rows.astype(jnp.bfloat16), 'row', axis_index_groups=a...  23.6 us
    all_to_all x1, blocking collectives, scatter_sum(): return jnp.sum(lax.all_to_all(parts, axis, 0, 0), axis=0)  23.5 us
    pallas_call x1, Pallas kernels, inverse_factor(): pl.pallas_call(inverse_factor_kernel, out_shape=jax.ShapeDtypeStruct((RAN...  18.3 us
    all_to_all x2, waiting for transfers between devices, exchange(): lax.all_to_all(jnp.broadcast_to(x, (size,) + x.shape), axis, 0, 0, axis_i...  16.4 us
    ppermute x3, starting transfers between devices, local(): lax.ppermute(packed, 'row', [(i, i ^ 2 * step) for i in range(n_row)])  10.8 us
    all_to_all x1, blocking collectives, exchange(): lax.all_to_all(jnp.broadcast_to(x, (size,) + x.shape), axis, 0, 0, axis_i...  10.6 us
    all_to_all x2, starting transfers between devices, exchange(): lax.all_to_all(jnp.broadcast_to(x, (size,) + x.shape), axis, 0, 0, axis_i...  7.13 us
    pallas_call x2, Pallas kernels, weights_half(): pl.pallas_call(weights_kernel, out_shape=jax.ShapeDtypeStruct((rows, RANK...  6.15 us
  transfers between devices with their start and end apart: 11, of which 8 were waited for; matrix products, arithmetic and copies ran while one was open for 4% of the time, Pallas kernels for 13%

profile of v2, /device:TPU:1, one launch (start us, length us, event | category | flops | bytes accessed | tf_op | source)
XLA Modules:
  0.0 177.8 jit_solution(16230905637078955309)
XLA Ops:
  7.2 0.0 copy-start
  7.2 2.5 %add_convert_fusion.b_ref = bf16[512,1664]{1,0:T(8,128)(2,1)S(1)} fusion(bf16[512,1664]{1,0:T(8,128)(2,1)} %param.4, bf16[512,1664]{1,0:T(8,128)(2,1)} %param.3), kind=kLoop, calls=%fused_computation.3 | loop fusion | flops 3407872 | bytes 5111808 | tf_op jit(solution)/shard_map/convert_element_type | solution.py:245
  9.7 0.0 copy-done
  9.7 0.0 copy-start.2
  9.7 1.1 fusion.2
  10.8 0.1 copy-done.2
  10.9 23.5 %all_to_all.20 = f32[16,32,512]{2,1,0:T(8,128)S(1)} all-to-all(f32[16,32,512]{2,1,0:T(8,128)S(1)} %bitcast.30), channel_id=1, replica_groups=mesh['row'=16,'col'=16] {'col'}, dimensions={0} | all-to-all | bytes 2097152 | tf_op jit(solution)/shard_map/all_to_all | solution.py:226
  34.4 0.1 reduce_sum.27
  34.4 1.1 broadcast_in_dim.10
  35.5 3.7 %all-to-all-start.1 = ((f32[16,32,512]{2,1,0:T(8,128)}), f32[16,32,512]{2,1,0:T(8,128)S(1)}, u32[]{:S(2)}, u32[]{:S(2)}) async-start(f32[16,32,512]{2,1,0:T(8,128)} %broadcast_in_dim.10), calls=%async_computation.1 | async-start | bytes 2097152 | tf_op jit(solution)/shard_map/all_to_all | solution.py:230
  39.2 0.0 reduce-scatter.2.cloned.1.call-start
  39.3 15.0 %all-to-all-done.1 = f32[16,32,512]{2,1,0:T(8,128)S(1)} async-done(((f32[16,32,512]{2,1,0:T(8,128)}), f32[16,32,512]{2,1,0:T(8,128)S(1)}, u32[]{:S(2)}, u32[]{:S(2)}) %all-to-all-start.1) | async-done | bytes 1048608 | tf_op jit(solution)/shard_map/all_to_all | solution.py:230
  54.3 0.0 copy-start.3
  54.3 1.5 copy-done.3
  55.7 2.9 %shard_map.58 = f32[832,512]{1,0:T(8,128)} custom-call(s32[1]{0:T(128)} %bitcast.half_ref, bf16[512,1664]{1,0:T(8,128)(2,1)S(1)} %copy-done.3, f32[512,512]{1,0:T(8,128)S(1)} %bitcast.22), custom_call_target="tpu_custom_call" | custom-call | flops 2147483648 | bytes 4194304 | tf_op jit(solution)/shard_map/pallas_call | solution.py:213
  58.6 3.3 %collective-permute-start.5 = (f32[832,512]{1,0:T(8,128)}, f32[832,512]{1,0:T(8,128)}, u32[]{:S(2)}, u32[]{:S(2)}) collective-permute-start(f32[832,512]{1,0:T(8,128)} %shard_map.58), channel_id=1, source_target_pairs={{0,16},{16,0},{32,48},{48,32},{64,80},{80,64},{96,112},{112,96},{1... | collective-permute-start | bytes 5111816 | tf_op jit(solution)/shard_map/ppermute | solution.py:251
  61.9 0.0 copy-start.4
  61.9 1.6 shard_map.59
  63.5 0.1 collective-permute-start
  63.6 1.8 %collective-permute-done.5.refs_0_ = f32[832,512]{1,0:T(8,128)} collective-permute-done((f32[832,512]{1,0:T(8,128)}, f32[832,512]{1,0:T(8,128)}, u32[]{:S(2)}, u32[]{:S(2)}) %collective-permute-start.5) | collective-permute-done | bytes 1703968 | tf_op jit(solution)/shard_map/ppermute | solution.py:251
  65.5 0.0 copy-done.4
  65.5 3.2 %shard_map.61 = f32[832,512]{1,0:T(8,128)S(1)} custom-call(s32[1]{0:T(128)} %bitcast.3.core_ref.half_ref, bf16[512,1664]{1,0:T(8,128)(2,1)S(1)} %copy-done.4, f32[512,512]{1,0:T(8,128)S(1)} %bitcast.24, f32[832,512]{1,0:T(8,128)} %collective-permute-done.5.refs_0_), custom_call_target="tpu_custom_call" | custom-call | flops 2147483648 | bytes 4194304 | tf_op jit(solution)/shard_map/pallas_call | solution.py:213
  68.7 0.0 copy-start.6
  68.7 1.2 copy-done.6
  69.9 0.0 reduce-scatter.2.cloned.1.call-update
  69.9 0.0 collective-permute-done
  70.0 1.7 collective-permute-start.1
  71.7 1.2 collective-permute-done.1
  72.9 3.0 %collective-permute-start.2 = (f32[40,128]{1,0:T(8,128)S(1)}, f32[40,128]{1,0:T(8,128)S(1)}, u32[]{:S(2)}, u32[]{:S(2)}) collective-permute-start(f32[40,128]{1,0:T(8,128)S(1)} %add.52), channel_id=1, source_target_pairs={{0,64},{16,80},{32,96},{48,112},{64,0},{80,16},{96,32},{112,48},{1... | collective-permute-start | bytes 61448 | tf_op jit(solution)/shard_map/ppermute | solution.py:267
  75.9 1.2 collective-permute-done.2
  77.1 6.1 %collective-permute-start.3 = (f32[40,128]{1,0:T(8,128)S(1)}, f32[40,128]{1,0:T(8,128)S(1)}, u32[]{:S(2)}, u32[]{:S(2)}) collective-permute-start(f32[40,128]{1,0:T(8,128)S(1)} %add.53), channel_id=1, source_target_pairs={{0,128},{16,144},{32,160},{48,176},{64,192},{80,208},{96,224},{112... | collective-permute-start | bytes 61448 | tf_op jit(solution)/shard_map/ppermute | solution.py:267
  83.1 1.2 collective-permute-done.3
  84.4 10.6 %all_to_all.21 = f32[16,40,128]{2,1,0:T(8,128)S(1)} all-to-all(f32[16,40,128]{2,1,0:T(8,128)S(1)} %broadcast_in_dim.11), channel_id=1, replica_groups=mesh['row'=16,'col'=16] {'col'}, dimensions={0} | all-to-all | bytes 655360 | tf_op jit(solution)/shard_map/all_to_all | solution.py:230
  95.0 5.1 %collective-permute-start.4 = (f32[5,128,128]{2,1,0:T(8,128)S(1)}, f32[5,128,128]{2,1,0:T(8,128)S(1)}, u32[]{:S(2)}, u32[]{:S(2)}) collective-permute-start(f32[5,128,128]{2,1,0:T(8,128)S(1)} %bitcast.26), channel_id=1, source_target_pairs={{0,16},{16,0},{32,48},{48,32},{64,80},{80,64},{96,112},{112,96},{1... | collective-permute-start | bytes 983048 | tf_op jit(solution)/shard_map/ppermute | solution.py:271
  100.0 1.3 collective-permute-done.4.theirs_ref
  101.3 18.3 %shard_map.60 = f32[512,512]{1,0:T(8,128)S(1)} custom-call(s32[1]{0:T(128)} %bitcast.3.core_ref.half_ref, f32[5,128,128]{2,1,0:T(8,128)S(1)} %bitcast.27, f32[5,128,128]{2,1,0:T(8,128)S(1)} %collective-permute-done.4.theirs_ref), custom_call_target="tpu_custom_call" | custom-call | flops 24999999488 | bytes 2097152 | tf_op jit(solution)/shard_map/pallas_call | solution.py:181
  119.6 0.0 copy-start.1
  119.6 1.0 copy-done.1
  120.6 1.9 %convolution_convert_fusion = bf16[512,512]{1,0:T(8,128)(2,1)S(1)} fusion(f32[512,512]{1,0:T(8,128)S(1)} %bitcast.25, f32[512,512]{1,0:T(8,128)S(1)} %shard_map.60), kind=kOutput, calls=%fused_computation.7 | convolution fusion | flops 1610874880 | bytes 2621440 | tf_op jit(solution)/shard_map/dot_general | solution.py:272
  122.5 0.0 reduce-scatter.2.cloned.1.call-done
  122.5 2.5 %convolution_convert_fusion.1 = bf16[104,512]{1,0:T(8,128)(2,1)S(1)} fusion(f32[104,512]{1,0:T(8,128)} %reduce-scatter.2.cloned.1.call-done, f32[512,512]{1,0:T(8,128)} %copy-done.1), kind=kOutput, calls=%fused_computation.8 | convolution fusion | flops 327208960 | bytes 1368064 | tf_op jit(solution)/shard_map/dot_general | solution.py:276
  125.0 23.6 %all_gather.3 = bf16[832,512]{1,0:T(8,128)(2,1)S(1)} all-gather(bf16[104,512]{1,0:T(8,128)(2,1)S(1)} %convolution_convert_fusion.1), channel_id=1, replica_groups={{0,32,64,96,128,160,192,224},{16,48,80,112,144,176,208,240},{1,33,65,97..., dimensions={0}, use_global_device_ids=true | all-gather | bytes 958464 | tf_op jit(solution)/shard_map/all_gather | solution.py:277
  148.6 5.5 %collective-permute-start.7 = (bf16[832,512]{1,0:T(8,128)(2,1)S(1)}, bf16[832,512]{1,0:T(8,128)(2,1)}, u32[]{:S(2)}, u32[]{:S(2)}) collective-permute-start(bf16[832,512]{1,0:T(8,128)(2,1)S(1)} %all_gather.3), channel_id=1, source_target_pairs={{0,16},{16,0},{32,48},{48,32},{64,80},{80,64},{96,112},{112,96},{1... | collective-permute-start | bytes 2555912 | tf_op jit(solution)/shard_map/ppermute | solution.py:242
  154.1 0.2 multiply_reduce_fusion
  154.4 0.1 collective-permute-start.6
  154.5 1.7 collective-permute-done.6
  156.1 0.6 broadcast_in_dim.12
  156.8 3.5 %all-to-all-start.3 = ((f32[16,4,128]{2,1,0:T(4,128)}), f32[16,4,128]{2,1,0:T(4,128)S(1)}, u32[]{:S(2)}, u32[]{:S(2)}) async-start(f32[16,4,128]{2,1,0:T(4,128)} %broadcast_in_dim.12), calls=%async_computation.4 | async-start | bytes 65536 | tf_op jit(solution)/shard_map/all_to_all | solution.py:230
  160.3 0.0 copy-start.5
  160.3 0.0 collective-permute-done.7
  160.3 1.4 broadcast_select_fusion.1
  161.7 0.0 copy-start.8
  161.7 0.0 copy-start.9
  161.7 0.9 copy-done.8
  162.6 0.3 copy-done.9
  162.9 0.0 copy-done.5
  162.9 2.4 %subtract_convert_fusion = bf16[512,1664]{1,0:T(8,128)(2,1)} fusion(bf16[512,1664]{1,0:T(8,128)(2,1)S(1)} %copy-done.5, bf16[512,512]{1,0:T(8,128)(2,1)S(1)} %convolution_convert_fusion, bf16[832,512]{1,0:T(8,128)(2,1)S(1)} %get-tuple-element.16, bf16[832,512]{1,0:T(8,128)(2,1)S(1)} %get-tuple-element.15), kind=kOutput, calls=%fused_computation.2 | convolution fusion | flops 879230976 | bytes 5636096 | tf_op jit(solution)/shard_map/dot_general | solution.py:284
  165.3 1.4 all-to-all-done.3
  166.7 1.9 %convert_multiply_fusion = f32[1664,512]{1,0:T(8,128)S(1)} fusion(f32[512]{0:T(512)S(1)} %rsqrt_bitcast_fusion, bf16[832,512]{1,0:T(8,128)(2,1)} %copy-done.9, bf16[832,512]{1,0:T(8,128)(2,1)} %copy-done.8), kind=kLoop, calls=%fused_computation.1 | loop fusion | flops 4259840 | bytes 5113856 | tf_op jit(solution)/shard_map/mul | solution.py:290
  168.6 0.0 copy-start.7
  168.6 2.3 %multiply_convert_fusion = bf16[512,1664]{1,0:T(8,128)(2,1)} fusion(bf16[512,512]{1,0:T(8,128)(2,1)S(1)} %convolution_convert_fusion, f32[1664,512]{1,0:T(8,128)S(1)} %convert_multiply_fusion), kind=kOutput, calls=%fused_computation | convolution fusion | flops 874971136 | bytes 5636096 | tf_op jit(solution)/shard_map/dot_general | solution.py:292
  170.9 0.0 copy-done.7
  (9 shorter events, 0.1 us)
Async XLA Ops:
  7.2 2.5 %copy-start = (bf16[1664,512]{1,0:T(8,128)(2,1)S(1)}, bf16[1664,512]{1,0:T(8,128)(2,1)}, u32[]{:S(2)}) copy-start(bf16[1664,512]{1,0:T(8,128)(2,1)} %param.5) | copy-start | bytes 5111812
  9.7 1.2 copy-start.2
  35.5 18.7 %all-to-all-start.1 = ((f32[16,32,512]{2,1,0:T(8,128)}), f32[16,32,512]{2,1,0:T(8,128)S(1)}, u32[]{:S(2)}, u32[]{:S(2)}) async-start(f32[16,32,512]{2,1,0:T(8,128)} %broadcast_in_dim.10), calls=%async_computation.1 | async-start | bytes 2097152 | tf_op jit(solution)/shard_map/all_to_all | solution.py:230
  39.2 83.3 %reduce-scatter.2.cloned.1.call-start = ((), (), s32[]{:S(2)}) async-start(), calls=%async_computation.5 | async-start | bytes 1916928 | tf_op jit(solution)/shard_map/reduce_scatter | solution.py:262
  54.3 1.5 copy-start.3
  58.6 6.9 %collective-permute-start.5 = (f32[832,512]{1,0:T(8,128)}, f32[832,512]{1,0:T(8,128)}, u32[]{:S(2)}, u32[]{:S(2)}) collective-permute-start(f32[832,512]{1,0:T(8,128)} %shard_map.58), channel_id=1, source_target_pairs={{0,16},{16,0},{32,48},{48,32},{64,80},{80,64},{96,112},{112,96},{1... | collective-permute-start | bytes 5111816 | tf_op jit(solution)/shard_map/ppermute | solution.py:251
  61.9 3.6 %copy-start.4 = (bf16[512,1664]{1,0:T(8,128)(2,1)S(1)}, bf16[512,1664]{1,0:T(8,128)(2,1)}, u32[]{:S(2)}) copy-start(bf16[512,1664]{1,0:T(8,128)(2,1)} %copy-done.2) | copy-start | bytes 5111812
  63.5 6.4 %collective-permute-start = (f32[40,128]{1,0:T(8,128)S(1)}, f32[40,128]{1,0:T(8,128)S(1)}, u32[]{:S(2)}, u32[]{:S(2)}) collective-permute-start(f32[40,128]{1,0:T(8,128)S(1)} %dynamic-slice_bitcast_fusion), channel_id=1, source_target_pairs={{0,16},{16,0},{32,48},{48,32},{64,80},{80,64},{96,112},{112,96},{1... | collective-permute-start | bytes 61448 | tf_op jit(solution)/shard_map/ppermute | solution.py:259
  68.7 1.2 copy-start.6
  70.0 2.9 %collective-permute-start.1 = (f32[40,128]{1,0:T(8,128)S(1)}, f32[40,128]{1,0:T(8,128)S(1)}, u32[]{:S(2)}, u32[]{:S(2)}) collective-permute-start(f32[40,128]{1,0:T(8,128)S(1)} %bitcast_add_fusion), channel_id=1, source_target_pairs={{0,32},{16,48},{32,0},{48,16},{64,96},{80,112},{96,64},{112,80},{1... | collective-permute-start | bytes 61448 | tf_op jit(solution)/shard_map/ppermute | solution.py:267
  72.9 4.2 %collective-permute-start.2 = (f32[40,128]{1,0:T(8,128)S(1)}, f32[40,128]{1,0:T(8,128)S(1)}, u32[]{:S(2)}, u32[]{:S(2)}) collective-permute-start(f32[40,128]{1,0:T(8,128)S(1)} %add.52), channel_id=1, source_target_pairs={{0,64},{16,80},{32,96},{48,112},{64,0},{80,16},{96,32},{112,48},{1... | collective-permute-start | bytes 61448 | tf_op jit(solution)/shard_map/ppermute | solution.py:267
  77.1 7.3 %collective-permute-start.3 = (f32[40,128]{1,0:T(8,128)S(1)}, f32[40,128]{1,0:T(8,128)S(1)}, u32[]{:S(2)}, u32[]{:S(2)}) collective-permute-start(f32[40,128]{1,0:T(8,128)S(1)} %add.53), channel_id=1, source_target_pairs={{0,128},{16,144},{32,160},{48,176},{64,192},{80,208},{96,224},{112... | collective-permute-start | bytes 61448 | tf_op jit(solution)/shard_map/ppermute | solution.py:267
  95.0 6.3 %collective-permute-start.4 = (f32[5,128,128]{2,1,0:T(8,128)S(1)}, f32[5,128,128]{2,1,0:T(8,128)S(1)}, u32[]{:S(2)}, u32[]{:S(2)}) collective-permute-start(f32[5,128,128]{2,1,0:T(8,128)S(1)} %bitcast.26), channel_id=1, source_target_pairs={{0,16},{16,0},{32,48},{48,32},{64,80},{80,64},{96,112},{112,96},{1... | collective-permute-start | bytes 983048 | tf_op jit(solution)/shard_map/ppermute | solution.py:271
  119.6 1.0 copy-start.1
  148.6 11.7 %collective-permute-start.7 = (bf16[832,512]{1,0:T(8,128)(2,1)S(1)}, bf16[832,512]{1,0:T(8,128)(2,1)}, u32[]{:S(2)}, u32[]{:S(2)}) collective-permute-start(bf16[832,512]{1,0:T(8,128)(2,1)S(1)} %all_gather.3), channel_id=1, source_target_pairs={{0,16},{16,0},{32,48},{48,32},{64,80},{80,64},{96,112},{112,96},{1... | collective-permute-start | bytes 2555912 | tf_op jit(solution)/shard_map/ppermute | solution.py:242
  154.4 1.8 collective-permute-start.6
  156.8 9.9 %all-to-all-start.3 = ((f32[16,4,128]{2,1,0:T(4,128)}), f32[16,4,128]{2,1,0:T(4,128)S(1)}, u32[]{:S(2)}, u32[]{:S(2)}) async-start(f32[16,4,128]{2,1,0:T(4,128)} %broadcast_in_dim.12), calls=%async_computation.4 | async-start | bytes 65536 | tf_op jit(solution)/shard_map/all_to_all | solution.py:230
  160.3 2.6 %copy-start.5 = (bf16[512,1664]{1,0:T(8,128)(2,1)S(1)}, bf16[512,1664]{1,0:T(8,128)(2,1)}, u32[]{:S(2)}) copy-start(bf16[512,1664]{1,0:T(8,128)(2,1)} %copy-done.2) | copy-start | bytes 5111812
  161.7 0.9 copy-start.8
  161.7 1.2 copy-start.9
  168.6 2.4 %copy-start.7 = (f32[1664,512]{1,0:T(8,128)}, f32[1664,512]{1,0:T(8,128)S(1)}, u32[]{:S(2)}) copy-start(f32[1664,512]{1,0:T(8,128)S(1)} %convert_multiply_fusion) | copy-start | bytes 10223620
Sparse Core Ops, SparseCore 0:
  70.1 36.4 reduce-scatter.1

commit v3 on v0

--- a/solution.py
+++ b/solution.py
@@ -172,7 +172,7 @@
         out_shape=jax.ShapeDtypeStruct((len(PAIRS), BLOCK, BLOCK), jnp.float32),
         in_specs=[pl.BlockSpec(memory_space=pltpu.VMEM)],
         out_specs=pl.BlockSpec(memory_space=pltpu.VMEM),
-        compiler_params=pltpu.CompilerParams(vmem_limit_bytes=16 * 1024 * 1024),
+        compiler_params=pltpu.CompilerParams(vmem_limit_bytes=14 * 1024 * 1024),
         cost_estimate=pl.CostEstimate(flops=2**31, bytes_accessed=2**21, transcendentals=0),
     )(projected)
 
@@ -189,7 +189,7 @@
             pltpu.VMEM((6 * BLOCK, RANK), jnp.bfloat16),
             pltpu.VMEM((6 * BLOCK, RANK), jnp.bfloat16),
         ],
-        compiler_params=pltpu.CompilerParams(vmem_limit_bytes=16 * 1024 * 1024),
+        compiler_params=pltpu.CompilerParams(vmem_limit_bytes=14 * 1024 * 1024),
         cost_estimate=pl.CostEstimate(flops=25 * 10**9, bytes_accessed=2**21, transcendentals=0),
     )(core.astype(jnp.int32).reshape(1), mine, theirs)
 
@@ -216,7 +216,7 @@
         in_specs=[pl.BlockSpec(memory_space=pltpu.SMEM)] + [vmem] * (2 + len(added)),
         out_specs=vmem,
         scratch_shapes=[pltpu.VMEM((blended.shape[1] - start, RANK), jnp.float32)],
-        compiler_params=pltpu.CompilerParams(vmem_limit_bytes=32 * 1024 * 1024),
+        compiler_params=pltpu.CompilerParams(vmem_limit_bytes=14 * 1024 * 1024),
         cost_estimate=pl.CostEstimate(flops=2**31, bytes_accessed=2**22, transcendentals=0),
     )(half.astype(jnp.int32).reshape(1), blended, projected, *added)
 

time: 176 us -> 176 us (level)
  no operation moved by 1% of the time
where the time goes in v3:
time: 176 us; the launch traced here: 175 us
  blocking collectives  55.1 us (31%)
  starting transfers between devices  31.1 us (18%)
  Pallas kernels  26.1 us (15%)
  waiting for transfers between devices  23.6 us (13%)
  between operations  14.3 us (8%)
  matrix products  10.2 us (6%)
  local copies, waits for them, and re-layouts  8.72 us (5%)
  other arithmetic  6.13 us (3%)
    all_to_all x1, blocking collectives, scatter_sum(): return jnp.sum(lax.all_to_all(parts, axis, 0, 0), axis=0)  23.5 us
    all_gather x1, blocking collectives, local(): lax.all_gather(back_rows.astype(jnp.bfloat16), 'row', axis_index_groups=a...  21 us
    all_to_all x3, waiting for transfers between devices, exchange(): lax.all_to_all(jnp.broadcast_to(x, (size,) + x.shape), axis, 0, 0, axis_i...  19.1 us
    all_to_all x3, starting transfers between devices, exchange(): lax.all_to_all(jnp.broadcast_to(x, (size,) + x.shape), axis, 0, 0, axis_i...  18.4 us
    pallas_call x1, Pallas kernels, inverse_factor(): pl.pallas_call(inverse_factor_kernel, out_shape=jax.ShapeDtypeStruct((RAN...  18.3 us
    all_to_all x1, blocking collectives, exchange(): lax.all_to_all(jnp.broadcast_to(x, (size,) + x.shape), axis, 0, 0, axis_i...  10.6 us
    unnamed x20, local copies, waits for them, and re-layouts  6.29 us
    pallas_call x2, Pallas kernels, weights_half(): pl.pallas_call(weights_kernel, out_shape=jax.ShapeDtypeStruct((rows, RANK...  6.15 us
  transfers between devices with their start and end apart: 9, of which 6 were waited for; matrix products, arithmetic and copies ran while one was open for 4% of the time, Pallas kernels for 13%

profile of v3, /device:TPU:1, one launch (start us, length us, event | category | flops | bytes accessed | tf_op | source)
XLA Modules:
  0.0 175.2 jit_solution(9052480618753705706)
XLA Ops:
  7.2 0.0 copy-start
  7.2 2.5 %add_convert_fusion.b_ref = bf16[512,1664]{1,0:T(8,128)(2,1)S(1)} fusion(bf16[512,1664]{1,0:T(8,128)(2,1)} %param.4, bf16[512,1664]{1,0:T(8,128)(2,1)} %param.3), kind=kLoop, calls=%fused_computation.3 | loop fusion | flops 3407872 | bytes 5111808 | tf_op jit(solution)/shard_map/convert_element_type | solution.py:245
  9.7 0.0 copy-done
  9.7 0.0 copy-start.2
  9.7 1.1 fusion.2
  10.8 0.1 copy-done.2
  10.9 23.5 %all_to_all.25 = f32[16,32,512]{2,1,0:T(8,128)S(1)} all-to-all(f32[16,32,512]{2,1,0:T(8,128)S(1)} %bitcast.30), channel_id=1, replica_groups=mesh['row'=16,'col'=16] {'col'}, dimensions={0} | all-to-all | bytes 2097152 | tf_op jit(solution)/shard_map/all_to_all | solution.py:226
  34.4 0.1 reduce_sum.36
  34.4 1.1 broadcast_in_dim.13
  35.5 3.7 %all-to-all-start.1 = ((f32[16,32,512]{2,1,0:T(8,128)}), f32[16,32,512]{2,1,0:T(8,128)S(1)}, u32[]{:S(2)}, u32[]{:S(2)}) async-start(f32[16,32,512]{2,1,0:T(8,128)} %broadcast_in_dim.13), calls=%async_computation.1 | async-start | bytes 2097152 | tf_op jit(solution)/shard_map/all_to_all | solution.py:230
  39.2 15.0 %all-to-all-done.1 = f32[16,32,512]{2,1,0:T(8,128)S(1)} async-done(((f32[16,32,512]{2,1,0:T(8,128)}), f32[16,32,512]{2,1,0:T(8,128)S(1)}, u32[]{:S(2)}, u32[]{:S(2)}) %all-to-all-start.1) | async-done | bytes 1048608 | tf_op jit(solution)/shard_map/all_to_all | solution.py:230
  54.3 0.0 copy-start.3
  54.3 1.5 copy-done.3
  55.7 2.9 %shard_map.58 = f32[832,512]{1,0:T(8,128)} custom-call(s32[1]{0:T(128)} %bitcast.half_ref, bf16[512,1664]{1,0:T(8,128)(2,1)S(1)} %copy-done.3, f32[512,512]{1,0:T(8,128)S(1)} %bitcast.22), custom_call_target="tpu_custom_call" | custom-call | flops 2147483648 | bytes 4194304 | tf_op jit(solution)/shard_map/pallas_call | solution.py:213
  58.6 3.3 %collective-permute-start.2 = (f32[832,512]{1,0:T(8,128)}, f32[832,512]{1,0:T(8,128)}, u32[]{:S(2)}, u32[]{:S(2)}) collective-permute-start(f32[832,512]{1,0:T(8,128)} %shard_map.58), channel_id=1, source_target_pairs={{0,16},{16,0},{32,48},{48,32},{64,80},{80,64},{96,112},{112,96},{1... | collective-permute-start | bytes 5111816 | tf_op jit(solution)/shard_map/ppermute | solution.py:251
  61.9 1.6 shard_map.59
  63.5 0.1 collective-permute-start
  63.6 1.5 collective-permute-done
  65.2 0.7 broadcast_in_dim.14
  65.9 8.2 %all-to-all-start.2 = ((f32[8,40,128]{2,1,0:T(8,128)}), f32[8,40,128]{2,1,0:T(8,128)S(1)}, u32[]{:S(2)}, u32[]{:S(2)}) async-start(f32[8,40,128]{2,1,0:T(8,128)} %broadcast_in_dim.14), calls=%async_computation.2 | async-start | bytes 327680 | tf_op jit(solution)/shard_map/all_to_all | solution.py:230
  74.0 0.0 reduce-scatter.2.cloned.1.call-start
  74.1 0.0 collective-permute-done.2.refs_0_
  74.1 0.0 copy-start.4
  74.1 1.4 copy-done.4
  75.6 3.2 %shard_map.61 = f32[832,512]{1,0:T(8,128)S(1)} custom-call(s32[1]{0:T(128)} %bitcast.3.core_ref.half_ref, bf16[512,1664]{1,0:T(8,128)(2,1)S(1)} %copy-done.4, f32[512,512]{1,0:T(8,128)S(1)} %bitcast.24, f32[832,512]{1,0:T(8,128)} %collective-permute-done.2.refs_0_), custom_call_target="tpu_custom_call" | custom-call | flops 2147483648 | bytes 4194304 | tf_op jit(solution)/shard_map/pallas_call | solution.py:213
  78.8 0.0 copy-start.6
  78.8 1.2 copy-done.6
  80.0 0.0 reduce-scatter.2.cloned.1.call-update
  80.0 2.6 %all-to-all-done.2 = f32[8,40,128]{2,1,0:T(8,128)S(1)} async-done(((f32[8,40,128]{2,1,0:T(8,128)}), f32[8,40,128]{2,1,0:T(8,128)S(1)}, u32[]{:S(2)}, u32[]{:S(2)}) %all-to-all-start.2) | async-done | bytes 163872 | tf_op jit(solution)/shard_map/all_to_all | solution.py:230
  82.7 10.6 %all_to_all.26 = f32[16,40,128]{2,1,0:T(8,128)S(1)} all-to-all(f32[16,40,128]{2,1,0:T(8,128)S(1)} %broadcast_in_dim.15), channel_id=1, replica_groups=mesh['row'=16,'col'=16] {'col'}, dimensions={0} | all-to-all | bytes 655360 | tf_op jit(solution)/shard_map/all_to_all | solution.py:230
  93.3 3.5 %collective-permute-start.1 = (f32[5,128,128]{2,1,0:T(8,128)S(1)}, f32[5,128,128]{2,1,0:T(8,128)S(1)}, u32[]{:S(2)}, u32[]{:S(2)}) collective-permute-start(f32[5,128,128]{2,1,0:T(8,128)S(1)} %bitcast.26), channel_id=1, source_target_pairs={{0,16},{16,0},{32,48},{48,32},{64,80},{80,64},{96,112},{112,96},{1... | collective-permute-start | bytes 983048 | tf_op jit(solution)/shard_map/ppermute | solution.py:268
  96.9 1.3 collective-permute-done.1.theirs_ref
  98.1 18.3 %shard_map.60 = f32[512,512]{1,0:T(8,128)S(1)} custom-call(s32[1]{0:T(128)} %bitcast.3.core_ref.half_ref, f32[5,128,128]{2,1,0:T(8,128)S(1)} %bitcast.27, f32[5,128,128]{2,1,0:T(8,128)S(1)} %collective-permute-done.1.theirs_ref), custom_call_target="tpu_custom_call" | custom-call | flops 24999999488 | bytes 2097152 | tf_op jit(solution)/shard_map/pallas_call | solution.py:181
  116.4 0.0 copy-start.1
  116.4 1.0 copy-done.1
  117.4 1.9 %convolution_convert_fusion = bf16[512,512]{1,0:T(8,128)(2,1)S(1)} fusion(f32[512,512]{1,0:T(8,128)S(1)} %bitcast.25, f32[512,512]{1,0:T(8,128)S(1)} %shard_map.60), kind=kOutput, calls=%fused_computation.7 | convolution fusion | flops 1610874880 | bytes 2621440 | tf_op jit(solution)/shard_map/dot_general | solution.py:269
  119.3 0.0 reduce-scatter.2.cloned.1.call-done
  119.3 2.5 %convolution_convert_fusion.1 = bf16[104,512]{1,0:T(8,128)(2,1)S(1)} fusion(f32[104,512]{1,0:T(8,128)} %reduce-scatter.2.cloned.1.call-done, f32[512,512]{1,0:T(8,128)} %copy-done.1), kind=kOutput, calls=%fused_computation.8 | convolution fusion | flops 327208960 | bytes 1368064 | tf_op jit(solution)/shard_map/dot_general | solution.py:273
  121.8 21.0 %all_gather.3 = bf16[832,512]{1,0:T(8,128)(2,1)S(1)} all-gather(bf16[104,512]{1,0:T(8,128)(2,1)S(1)} %convolution_convert_fusion.1), channel_id=1, replica_groups={{0,32,64,96,128,160,192,224},{16,48,80,112,144,176,208,240},{1,33,65,97..., dimensions={0}, use_global_device_ids=true | all-gather | bytes 958464 | tf_op jit(solution)/shard_map/all_gather | solution.py:274
  142.8 5.7 %collective-permute-start.4 = (bf16[832,512]{1,0:T(8,128)(2,1)S(1)}, bf16[832,512]{1,0:T(8,128)(2,1)}, u32[]{:S(2)}, u32[]{:S(2)}) collective-permute-start(bf16[832,512]{1,0:T(8,128)(2,1)S(1)} %all_gather.3), channel_id=1, source_target_pairs={{0,16},{16,0},{32,48},{48,32},{64,80},{80,64},{96,112},{112,96},{1... | collective-permute-start | bytes 2555912 | tf_op jit(solution)/shard_map/ppermute | solution.py:242
  148.5 0.2 multiply_reduce_fusion
  148.7 0.1 collective-permute-start.3
  148.8 1.7 collective-permute-done.3
  150.5 0.6 broadcast_in_dim.16
  151.1 6.5 %all-to-all-start.4 = ((f32[16,4,128]{2,1,0:T(4,128)}), f32[16,4,128]{2,1,0:T(4,128)S(1)}, u32[]{:S(2)}, u32[]{:S(2)}) async-start(f32[16,4,128]{2,1,0:T(4,128)} %broadcast_in_dim.16), calls=%async_computation.5 | async-start | bytes 65536 | tf_op jit(solution)/shard_map/all_to_all | solution.py:230
  157.6 0.0 copy-start.5
  157.6 0.0 collective-permute-done.4
  157.6 1.4 broadcast_select_fusion.1
  159.0 0.0 copy-start.8
  159.0 0.0 copy-start.9
  159.0 0.9 copy-done.8
  160.0 0.2 copy-done.9
  160.2 0.0 copy-done.5
  160.2 2.4 %subtract_convert_fusion = bf16[512,1664]{1,0:T(8,128)(2,1)} fusion(bf16[512,1664]{1,0:T(8,128)(2,1)S(1)} %copy-done.5, bf16[512,512]{1,0:T(8,128)(2,1)S(1)} %convolution_convert_fusion, bf16[832,512]{1,0:T(8,128)(2,1)S(1)} %get-tuple-element.16, bf16[832,512]{1,0:T(8,128)(2,1)S(1)} %get-tuple-element.15), kind=kOutput, calls=%fused_computation.2 | convolution fusion | flops 879230976 | bytes 5636096 | tf_op jit(solution)/shard_map/dot_general | solution.py:281
  162.6 1.4 all-to-all-done.4
  164.1 1.9 %convert_multiply_fusion = f32[1664,512]{1,0:T(8,128)S(1)} fusion(f32[512]{0:T(512)S(1)} %rsqrt_bitcast_fusion, bf16[832,512]{1,0:T(8,128)(2,1)} %copy-done.9, bf16[832,512]{1,0:T(8,128)(2,1)} %copy-done.8), kind=kLoop, calls=%fused_computation.1 | loop fusion | flops 4259840 | bytes 5113856 | tf_op jit(solution)/shard_map/mul | solution.py:287
  166.0 0.0 copy-start.7
  166.0 2.3 %multiply_convert_fusion = bf16[512,1664]{1,0:T(8,128)(2,1)} fusion(bf16[512,512]{1,0:T(8,128)(2,1)S(1)} %convolution_convert_fusion, f32[1664,512]{1,0:T(8,128)S(1)} %convert_multiply_fusion), kind=kOutput, calls=%fused_computation | convolution fusion | flops 874971136 | bytes 5636096 | tf_op jit(solution)/shard_map/dot_general | solution.py:289
  168.3 0.0 copy-done.7
  (7 shorter events, 0.1 us)
Async XLA Ops:
  7.2 2.5 %copy-start = (bf16[1664,512]{1,0:T(8,128)(2,1)S(1)}, bf16[1664,512]{1,0:T(8,128)(2,1)}, u32[]{:S(2)}) copy-start(bf16[1664,512]{1,0:T(8,128)(2,1)} %param.5) | copy-start | bytes 5111812
  9.7 1.2 copy-start.2
  35.5 18.7 %all-to-all-start.1 = ((f32[16,32,512]{2,1,0:T(8,128)}), f32[16,32,512]{2,1,0:T(8,128)S(1)}, u32[]{:S(2)}, u32[]{:S(2)}) async-start(f32[16,32,512]{2,1,0:T(8,128)} %broadcast_in_dim.13), calls=%async_computation.1 | async-start | bytes 2097152 | tf_op jit(solution)/shard_map/all_to_all | solution.py:230
  54.3 1.5 copy-start.3
  58.6 15.5 %collective-permute-start.2 = (f32[832,512]{1,0:T(8,128)}, f32[832,512]{1,0:T(8,128)}, u32[]{:S(2)}, u32[]{:S(2)}) collective-permute-start(f32[832,512]{1,0:T(8,128)} %shard_map.58), channel_id=1, source_target_pairs={{0,16},{16,0},{32,48},{48,32},{64,80},{80,64},{96,112},{112,96},{1... | collective-permute-start | bytes 5111816 | tf_op jit(solution)/shard_map/ppermute | solution.py:251
  63.5 1.6 collective-permute-start
  65.9 16.8 %all-to-all-start.2 = ((f32[8,40,128]{2,1,0:T(8,128)}), f32[8,40,128]{2,1,0:T(8,128)S(1)}, u32[]{:S(2)}, u32[]{:S(2)}) async-start(f32[8,40,128]{2,1,0:T(8,128)} %broadcast_in_dim.14), calls=%async_computation.2 | async-start | bytes 327680 | tf_op jit(solution)/shard_map/all_to_all | solution.py:230
  74.0 45.3 %reduce-scatter.2.cloned.1.call-start = ((), (), s32[]{:S(2)}) async-start(), calls=%async_computation.6 | async-start | bytes 1916928 | tf_op jit(solution)/shard_map/reduce_scatter | solution.py:262
  74.1 1.5 copy-start.4
  78.8 1.2 copy-start.6
  93.3 4.8 %collective-permute-start.1 = (f32[5,128,128]{2,1,0:T(8,128)S(1)}, f32[5,128,128]{2,1,0:T(8,128)S(1)}, u32[]{:S(2)}, u32[]{:S(2)}) collective-permute-start(f32[5,128,128]{2,1,0:T(8,128)S(1)} %bitcast.26), channel_id=1, source_target_pairs={{0,16},{16,0},{32,48},{48,32},{64,80},{80,64},{96,112},{112,96},{1... | collective-permute-start | bytes 983048 | tf_op jit(solution)/shard_map/ppermute | solution.py:268
  116.4 1.0 copy-start.1
  142.8 14.8 %collective-permute-start.4 = (bf16[832,512]{1,0:T(8,128)(2,1)S(1)}, bf16[832,512]{1,0:T(8,128)(2,1)}, u32[]{:S(2)}, u32[]{:S(2)}) collective-permute-start(bf16[832,512]{1,0:T(8,128)(2,1)S(1)} %all_gather.3), channel_id=1, source_target_pairs={{0,16},{16,0},{32,48},{48,32},{64,80},{80,64},{96,112},{112,96},{1... | collective-permute-start | bytes 2555912 | tf_op jit(solution)/shard_map/ppermute | solution.py:242
  148.7 1.8 %collective-permute-start.3 = (f32[4,128]{1,0:T(4,128)S(1)}, f32[4,128]{1,0:T(4,128)S(1)}, u32[]{:S(2)}, u32[]{:S(2)}) collective-permute-start(f32[4,128]{1,0:T(4,128)S(1)} %bitcast.31), channel_id=1, source_target_pairs={{0,16},{16,0},{32,48},{48,32},{64,80},{80,64},{96,112},{112,96},{1... | collective-permute-start | bytes 6152 | tf_op jit(solution)/shard_map/ppermute | solution.py:278
  151.1 13.0 %all-to-all-start.4 = ((f32[16,4,128]{2,1,0:T(4,128)}), f32[16,4,128]{2,1,0:T(4,128)S(1)}, u32[]{:S(2)}, u32[]{:S(2)}) async-start(f32[16,4,128]{2,1,0:T(4,128)} %broadcast_in_dim.16), calls=%async_computation.5 | async-start | bytes 65536 | tf_op jit(solution)/shard_map/all_to_all | solution.py:230
  157.6 2.6 %copy-start.5 = (bf16[512,1664]{1,0:T(8,128)(2,1)S(1)}, bf16[512,1664]{1,0:T(8,128)(2,1)}, u32[]{:S(2)}) copy-start(bf16[512,1664]{1,0:T(8,128)(2,1)} %copy-done.2) | copy-start | bytes 5111812
  159.0 0.9 copy-start.8
  159.0 1.2 copy-start.9
  166.0 2.4 %copy-start.7 = (f32[1664,512]{1,0:T(8,128)}, f32[1664,512]{1,0:T(8,128)S(1)}, u32[]{:S(2)}) copy-start(f32[1664,512]{1,0:T(8,128)S(1)} %convert_multiply_fusion) | copy-start | bytes 10223620
Sparse Core Ops, SparseCore 0:
  80.1 34.6 reduce-scatter.1
